TPU v7x, 32 devices: a whole 2x2x4 slice. The times are simulated.
32 devices in a mesh: dp: 8 (over y, x, core), tensor: 4 (over z).
Axes of the slice: x: 2, y: 2, z: 4, core: 2. Of those that a mesh axis runs over, the one named last changes fastest.
Arguments:
- block_input: bfloat16 [16, 2048, 768], P('dp', 'tensor'), may hold values from -6 to 6
- norm_gain: float32 [768], replicated, may hold values from 0.5 to 1.5
- input_gate_inner_weight: bfloat16 [768, 2, 1536], P('dp', None, 'tensor'), may hold values from -0.21875 to 0.21875
- input_shared_weight: bfloat16 [768, 256], P('dp'), may hold values from -0.21875 to 0.21875
- input_delta_weight: bfloat16 [768, 24], P('dp', 'tensor'), may hold values from -0.21875 to 0.21875
- conv_inner: bfloat16 [4, 1536], P(None, 'tensor'), may hold values from -3 to 3
- shift_inner: bfloat16 [1536], P('tensor'), may hold values from -3 to 3
- conv_shared: bfloat16 [4, 256], replicated, may hold values from -3 to 3
- shift_shared: bfloat16 [256], replicated, may hold values from -3 to 3
- decay_log: float32 [24], P('tensor'), may hold values from 0 to 2.77
- delta_bias: float32 [24], P('tensor'), may hold values from -6.9 to -2.3
- skip_gain: float32 [24], P('tensor'), may hold values from 0.5 to 1.5
- gated_gain: float32 [1536], P('tensor'), may hold values from 0.5 to 1.5
- output_projection_weight: bfloat16 [1536, 768], P('tensor', 'dp'), may hold values from -0.15625 to 0.15625
- cotangent: bfloat16 [16, 2048, 768], P('dp', 'tensor'), may hold values from -6 to 6
Outputs:
- block_output: bfloat16 [16, 2048, 768], P('dp', 'tensor')
- input_grad: bfloat16 [16, 2048, 768], P('dp', 'tensor')
- norm_gain_grad: float32 [768], replicated
- gate_inner_grad: float32 [768, 2, 1536], P('dp', None, 'tensor')
- shared_bc_grad: float32 [768, 256], P('dp')
- delta_grad: float32 [768, 24], P('dp', 'tensor')
- conv_inner_grad: float32 [4, 1536], P(None, 'tensor')
- shift_inner_grad: float32 [1536], P('tensor')
- conv_shared_grad: float32 [4, 256], replicated
- shift_shared_grad: float32 [256], replicated
- decay_log_grad: float32 [24], P('tensor')
- delta_bias_grad: float32 [24], P('tensor')
- bypass_factor_sensitivity: float32 [24], P('tensor')
- gated_gain_grad: float32 [1536], P('tensor')
- out_weight_grad: float32 [1536, 768], P('tensor', 'dp')
All inputs are finite; a program needn't handle non-finite values.
Results may differ from a plain program's by a relative error of at most 0.0095.
Values may be sent and summed in bfloat16 or wider, within the bound.
A program may use at most 320 MiB of HBM per device.

v0:
```python
import math

import jax
import jax.numpy as jnp
from jax import lax
from jax.sharding import PartitionSpec as P

P_SIZE = 64
SPAN = 256


EPSILON = 1e-05
TOP_PRECISION = lax.Precision.HIGHEST


def in_blocks(x, dim, peers):
    dims = x.shape
    tiles = x.reshape(*dims[:dim], peers, dims[dim] // peers, *dims[dim + 1 :])
    return jnp.moveaxis(tiles, dim, 0)


def sum_at_owner(x, axis, dim):
    peers = lax.axis_size(axis)
    tiles = lax.all_to_all(in_blocks(x, dim, peers), axis, 0, 0, tiled=True)
    return jnp.sum(tiles.astype(jnp.float32), axis=0)


def in_one_piece(arrays, axis, dim, along):
    widths = [math.prod(a.shape[along:]) for a in arrays]
    both = jnp.concatenate(
        [a.reshape(*a.shape[:along], w) for a, w in zip(arrays, widths)], axis=along
    )
    whole = sum_at_owner(both, axis, dim)
    tiles = jnp.split(whole, [sum(widths[:k]) for k in range(1, len(widths))], axis=along)
    return tuple((b.reshape(*whole.shape[:along], *a.shape[along:]) for a, b in zip(arrays, tiles)))


def causal_conv(values, kernel, offset):
    taps = kernel.shape[0]
    seq_length = values.shape[1]
    padded = jnp.pad(values, ((0, 0), (taps - 1, 0), (0, 0)))
    running = offset + jnp.zeros_like(values)
    for tap_index in range(taps):
        running = running + padded[:, tap_index : tap_index + seq_length, :] * kernel[tap_index]
    return running


def block_mixing(shared_seq):
    state_dim = shared_seq.shape[-1] // 2
    block_count = shared_seq.shape[0] // SPAN
    blocked_b = shared_seq[:, :state_dim].reshape(block_count, SPAN, state_dim)
    readout_matrix_tiles = shared_seq[:, state_dim:].reshape(block_count, SPAN, state_dim)
    return jnp.einsum(
        "ctn,csn->cts", readout_matrix_tiles, blocked_b, preferred_element_type=jnp.float32
    )


def scan_heads(inner_act, delta, decay_log, b_values, c_values, mixing, skip_gain, block, head_dim):
    seq_length = inner_act.shape[0]
    head_count = delta.shape[1]
    block_count = seq_length // block
    decay_rate = -jnp.exp(decay_log)
    blocked_x = inner_act.reshape(block_count, block, head_count, head_dim)
    blocked_dt = delta.reshape(block_count, block, head_count)
    blocked_b = b_values.reshape(block_count, block, -1)
    readout_matrix_tiles = c_values.reshape(block_count, block, -1)
    log_decay = jnp.cumsum(blocked_dt * decay_rate, axis=1)
    spread = log_decay[:, :, None, :] - log_decay[:, None, :, :]
    lower = (jnp.arange(block)[:, None] >= jnp.arange(block)[None, :])[None, :, :, None]
    decay_mat = jnp.where(lower, jnp.exp(jnp.where(lower, spread, 0.0)), 0.0)
    scores = mixing[:, :, :, None] * decay_mat * blocked_dt[:, None, :, :]
    intra_segment_term = jnp.einsum("ctsh,cshp->cthp", scores, blocked_x, precision=TOP_PRECISION)
    to_end = jnp.exp(log_decay[:, -1:, :] - log_decay) * blocked_dt
    fresh_states = jnp.einsum(
        "csn,csh,cshp->chnp", blocked_b, to_end, blocked_x, precision=TOP_PRECISION
    )
    block_decay = jnp.exp(log_decay[:, -1, :])

    def advance(carried, scan_item):
        factor, fresh = scan_item
        return (factor[:, None, None] * carried + fresh, carried)

    initial = jnp.zeros(fresh_states.shape[1:], fresh_states.dtype)
    final_state, entering = lax.scan(advance, initial, (block_decay, fresh_states))
    across = (
        jnp.einsum("ctn,chnp->cthp", readout_matrix_tiles, entering, precision=TOP_PRECISION)
        * jnp.exp(log_decay)[..., None]
    )
    result = intra_segment_term + across + skip_gain[None, None, :, None] * blocked_x
    return result.reshape(seq_length, head_count * head_dim)


def conv_piece(
    inner_raw, shared_before_activation, conv_inner, shift_inner, conv_shared, shift_shared
):
    return (
        jax.nn.silu(causal_conv(inner_raw, conv_inner, shift_inner)),
        jax.nn.silu(causal_conv(shared_before_activation, conv_shared, shift_shared)),
    )


def mixer_piece(
    inner_act, delta_before_softplus, shared_act, mixing, gate_raw, decay_log, delta_bias, skip_gain
):
    state_dim = shared_act.shape[-1] // 2
    delta = jax.nn.softplus(delta_before_softplus + delta_bias)
    mixed = scan_heads(
        inner_act,
        delta,
        decay_log,
        shared_act[:, :state_dim],
        shared_act[:, state_dim:],
        mixing,
        skip_gain,
        SPAN,
        P_SIZE,
    )
    return mixed * jax.nn.silu(gate_raw)


def local(
    block_input,
    norm_gain,
    input_gate_inner_weight,
    input_shared_weight,
    input_delta_weight,
    conv_inner,
    shift_inner,
    conv_shared,
    shift_shared,
    decay_log,
    delta_bias,
    skip_gain,
    gated_gain,
    output_projection_weight,
    cotangent,
):
    local_in = block_input.astype(jnp.float32)
    inv_root = lax.rsqrt(jnp.mean(local_in * local_in, axis=-1, keepdims=True) + EPSILON)
    normalized_local_rows = (local_in * inv_root * norm_gain).astype(jnp.bfloat16)
    rescaled_token_vectors = lax.all_gather(normalized_local_rows, "tensor", axis=1, tiled=True)
    weights_all = (
        lax.all_gather(input_gate_inner_weight, "dp", axis=0, tiled=True),
        lax.all_gather(input_shared_weight, "dp", axis=0, tiled=True),
        lax.all_gather(input_delta_weight, "dp", axis=0, tiled=True),
        lax.all_gather(output_projection_weight, "dp", axis=1, tiled=True),
    )
    gate_inner_full, shared_gathered_rows, delta_gathered_rows, output_gathered_rows = weights_all
    model_channel_count = gate_inner_full.shape[0]
    inner_local = gate_inner_full.shape[2]
    tensor_count = lax.axis_size("tensor")
    inner_total = inner_local * tensor_count
    projected_output_rows = jnp.einsum(
        "kaf,ft->kat",
        rescaled_token_vectors,
        gate_inner_full.reshape(model_channel_count, 2 * inner_local),
        preferred_element_type=jnp.float32,
    )
    gate_raw = projected_output_rows[..., :inner_local]
    inner_raw = projected_output_rows[..., inner_local:]
    shared_before_activation = jnp.einsum(
        "kaf,ft->kat",
        rescaled_token_vectors,
        shared_gathered_rows,
        preferred_element_type=jnp.float32,
    )
    delta_before_softplus = jnp.einsum(
        "jct,ti->jci",
        rescaled_token_vectors,
        delta_gathered_rows,
        preferred_element_type=jnp.float32,
    )
    conv_params = (
        conv_inner.astype(jnp.float32),
        shift_inner.astype(jnp.float32),
        conv_shared.astype(jnp.float32),
        shift_shared.astype(jnp.float32),
    )
    conv_values, conv_pull = jax.vjp(conv_piece, inner_raw, shared_before_activation, *conv_params)
    inner_act = conv_values[0].astype(jnp.bfloat16)
    shared_act = conv_values[1].astype(jnp.bfloat16)

    def run_sequence(seq_item):
        inner_seq, delta_seq, shared_seq, gate_seq = seq_item
        mixing = block_mixing(shared_seq)
        return mixer_piece(
            inner_seq.astype(jnp.float32),
            delta_seq,
            shared_seq.astype(jnp.float32),
            mixing,
            gate_seq,
            decay_log,
            delta_bias,
            skip_gain,
        )

    gated = lax.map(run_sequence, (inner_act, delta_before_softplus, shared_act, gate_raw))
    square_sum = lax.psum(jnp.sum(gated * gated, axis=-1), "tensor")
    inv_gate = lax.rsqrt(square_sum / inner_total + EPSILON)[..., None]
    mixer_output_rows = (gated * inv_gate * gated_gain).astype(jnp.bfloat16)
    partial_output_rows = jnp.einsum(
        "gue,ea->gua", mixer_output_rows, output_gathered_rows, preferred_element_type=jnp.float32
    )
    branch = lax.psum_scatter(
        partial_output_rows.astype(jnp.bfloat16), "tensor", scatter_dimension=1, tiled=True
    ).astype(jnp.float32)
    block_output = (local_in + branch).astype(jnp.bfloat16)
    gate_inner_back, shared_pullback_rows, delta_pullback_rows, output_pullback_rows = (
        lax.all_gather(input_gate_inner_weight, "dp", axis=0, tiled=True),
        lax.all_gather(input_shared_weight, "dp", axis=0, tiled=True),
        lax.all_gather(input_delta_weight, "dp", axis=0, tiled=True),
        lax.all_gather(output_projection_weight, "dp", axis=1, tiled=True),
    )
    complete_cotangent = lax.all_gather(cotangent, "tensor", axis=1, tiled=True)
    out_grad_local = jnp.einsum(
        "oef,oeg->fg", mixer_output_rows, complete_cotangent, preferred_element_type=jnp.float32
    )
    mixer_output_gradient = jnp.einsum(
        "qfk,zk->qfz", complete_cotangent, output_pullback_rows, preferred_element_type=jnp.float32
    )
    gated_gain_grad = jnp.sum(mixer_output_gradient * gated * inv_gate, axis=(0, 1))
    scaled = mixer_output_gradient * gated_gain
    inner_prod = lax.psum(jnp.sum(scaled * gated, axis=-1), "tensor")
    gated_grad = (
        inv_gate * scaled
        - gated * (inv_gate * inv_gate * inv_gate) * (inner_prod / inner_total)[..., None]
    )

    def back_sequence(seq_item):
        inner_seq, delta_seq, shared_seq, gate_seq, grad_seq = seq_item
        mixing = block_mixing(shared_seq)
        shared_float = shared_seq.astype(jnp.float32)
        primal, pullback = jax.vjp(
            mixer_piece,
            inner_seq.astype(jnp.float32),
            delta_seq,
            shared_float,
            mixing,
            gate_seq,
            decay_log,
            delta_bias,
            skip_gain,
        )
        inner_g, delta_g, shared_g, mixing_g, gate_g, decay_g, bias_g, skip_g = pullback(grad_seq)
        state_dim = shared_float.shape[-1] // 2
        block_count = shared_float.shape[0] // SPAN
        blocked_b = shared_float[:, :state_dim].reshape(block_count, SPAN, state_dim)
        readout_matrix_tiles = shared_float[:, state_dim:].reshape(block_count, SPAN, state_dim)
        readout_matrix_spare = jnp.einsum(
            "cts,csn->ctn", mixing_g, blocked_b, precision=TOP_PRECISION
        )
        b_extra = jnp.einsum(
            "cts,ctn->csn", mixing_g, readout_matrix_tiles, precision=TOP_PRECISION
        )
        extra = jnp.concatenate(
            [b_extra.reshape(-1, state_dim), readout_matrix_spare.reshape(-1, state_dim)], axis=-1
        )
        return (inner_g, delta_g, shared_g + extra, gate_g, decay_g, bias_g, skip_g)

    seq_grads = lax.map(
        back_sequence, (inner_act, delta_before_softplus, shared_act, gate_raw, gated_grad)
    )
    (
        inner_act_grad,
        delta_raw_grad,
        shared_act_grad,
        gate_raw_grad,
        decay_parts,
        bias_parts,
        skip_parts,
    ) = seq_grads
    decay_log_grad = jnp.sum(decay_parts, axis=0)
    delta_bias_grad = jnp.sum(bias_parts, axis=0)
    bypass_factor_sensitivity = jnp.sum(skip_parts, axis=0)
    (
        inner_raw_grad,
        shared_raw_grad,
        conv_inner_grad,
        shift_inner_grad,
        conv_shared_grad,
        shift_shared_grad,
    ) = conv_pull((inner_act_grad, shared_act_grad))
    gate_inner_low_precision = jnp.concatenate([gate_raw_grad, inner_raw_grad], axis=-1).astype(
        jnp.bfloat16
    )
    step_size_reduced_bits = delta_raw_grad.astype(jnp.bfloat16)
    gate_inner_part = jnp.einsum(
        "hmu,hmx->ux",
        rescaled_token_vectors,
        gate_inner_low_precision,
        preferred_element_type=jnp.float32,
    ).reshape(model_channel_count, 2, inner_local)
    delta_part = jnp.einsum(
        "ubp,ubd->pd",
        rescaled_token_vectors,
        step_size_reduced_bits,
        preferred_element_type=jnp.float32,
    )
    normed_grad = jnp.einsum(
        "urt,kt->urk",
        gate_inner_low_precision,
        gate_inner_back.reshape(model_channel_count, 2 * inner_local),
        preferred_element_type=jnp.float32,
    )
    normed_grad = normed_grad + jnp.einsum(
        "iaz,bz->iab",
        step_size_reduced_bits,
        delta_pullback_rows,
        preferred_element_type=jnp.float32,
    )
    local_grad, shared_local_grad = (
        lax.psum_scatter(normed_grad, "tensor", scatter_dimension=1, tiled=True),
        lax.psum_scatter(shared_raw_grad, "tensor", scatter_dimension=1, tiled=True),
    )
    shared_low_precision = shared_local_grad.astype(jnp.bfloat16)
    local_grad = local_grad + jnp.einsum(
        "fnw,kw->fnk",
        shared_low_precision,
        shared_pullback_rows,
        preferred_element_type=jnp.float32,
    )
    shared_part = jnp.einsum(
        "tqm,tqu->mu",
        normalized_local_rows,
        shared_low_precision,
        preferred_element_type=jnp.float32,
    )
    norm_gain_grad = jnp.sum(local_grad * local_in * inv_root, axis=(0, 1))
    scaled_in = local_grad * norm_gain
    input_grad = (
        cotangent.astype(jnp.float32)
        + inv_root * scaled_in
        - local_in
        * (inv_root * inv_root * inv_root)
        * jnp.mean(scaled_in * local_in, axis=-1, keepdims=True)
    ).astype(jnp.bfloat16)
    gate_inner_grad, shared_sliced, delta_grad, out_weight_grad = (
        *in_one_piece(
            (
                gate_inner_part.astype(jnp.bfloat16),
                shared_part.astype(jnp.bfloat16),
                delta_part.astype(jnp.bfloat16),
            ),
            "dp",
            0,
            1,
        ),
        sum_at_owner(out_grad_local.astype(jnp.bfloat16), "dp", 1),
    )
    segment_subtotals = lax.psum(
        (
            conv_inner_grad,
            shift_inner_grad,
            decay_log_grad,
            delta_bias_grad,
            bypass_factor_sensitivity,
            gated_gain_grad,
            conv_shared_grad,
            shift_shared_grad,
            norm_gain_grad,
        ),
        "dp",
    )
    shared_sums = lax.psum(
        (shared_sliced, segment_subtotals[6], segment_subtotals[7], segment_subtotals[8]), "tensor"
    )
    return (
        block_output,
        input_grad,
        shared_sums[3],
        gate_inner_grad,
        shared_sums[0],
        delta_grad,
        segment_subtotals[0],
        segment_subtotals[1],
        shared_sums[1],
        shared_sums[2],
        segment_subtotals[2],
        segment_subtotals[3],
        segment_subtotals[4],
        segment_subtotals[5],
        out_weight_grad,
    )


def solution(mesh):
    placed = (
        P("dp", "tensor", None),
        P(),
        P("dp", None, "tensor"),
        P("dp", None),
        P("dp", "tensor"),
        P(None, "tensor"),
        P("tensor"),
        P(),
        P(),
        P("tensor"),
        P("tensor"),
        P("tensor"),
        P("tensor"),
        P("tensor", "dp"),
        P("dp", "tensor", None),
    )
    return jax.shard_map(
        local,
        mesh=mesh,
        in_specs=placed,
        out_specs=(
            P("dp", "tensor", None),
            P("dp", "tensor", None),
            P(),
            P("dp", None, "tensor"),
            P("dp", None),
            P("dp", "tensor"),
            P(None, "tensor"),
            P("tensor"),
            P(),
            P(),
            P("tensor"),
            P("tensor"),
            P("tensor"),
            P("tensor"),
            P("tensor", "dp"),
        ),
        check_vma=False,
    )
```

profile of v0, /device:TPU:0, one launch (start us, length us, event | category | flops | bytes accessed | tf_op | source)
XLA Modules:
  0.0 1478.5 jit_solution(30850938930884416)
XLA Ops:
  26.2 10.8 all_gather.24
  50.5 104.8 %all-gather.5.cloned.1.call-done = bf16[2,2048,768]{2,1,0:T(8,128)(2,1)} async-done(((bf16[2,512,768]{2,1,0:T(8,128)(2,1)}), bf16[2,2048,768]{2,1,0:T(8,128)(2,1)}) %all-gather.5.cloned.1.call-update) | async-done | bytes 6291472 | tf_op jit(solution)/shard_map/all_gather | solution.py:141
  182.9 15.0 %multiply_convert_fusion.1 = (bf16[2,2048,384]{2,1,0:T(8,128)(2,1)}, f32[2,2048,384]{2,1,0:T(8,128)}) fusion(f32[2,2048,384]{2,1,0:T(8,128)} %get-tuple-element.1195, f32[384]{0:T(512)S(1)} %get-tuple-element.1063, f32[384]{0:T(512)S(1)} %get-tuple-element.1064, f32[384]{0:T(512)S(1)} %get-tuple-element.1065, f32[384]{0:T(512)S(1)} %get-tuple-element.1062, ...), kind=kLoop, calls=%fused_computation.190 | loop fusion | flops 20447232 | bytes 15736320 | tf_op jit(solution)/shard_map/convert_element_type | solution.py:180
  214.1 104.3 %while.124 = (s32[]{:T(128)}, f32[2,2048,384]{1,2,0:T(8,128)}, bf16[2,2048,384]{1,2,0:T(8,128)(2,1)}, bf16[2,2048,256]{2,1,0:T(8,128)(2,1)}, f32[2,2048,6]{1,2,0...) while((s32[]{:T(128)}, f32[2,2048,384]{1,2,0:T(8,128)}, ...), condition=%wide.region_6.7_spmd, body=%wide.region_1.6_spmd.sunk | while | flops 4993142784 | bytes 73489480 | solution.py:197
  226.0 16.7 %while.128 = (s32[]{:T(128)}, f32[6,128,64]{2,1,0:T(8,128)S(1)}, f32[8,6,128,64]{2,3,1,0:T(8,128)}, f32[8,6]{1,0:T(8,128)S(1)}, f32[8,6,128,64]{2,3,1,0:T(8,128)}, /*index=5*/s32[]{:T(128)}, s32[]{:T(128)}) while((s32[]{:T(128)}, f32[6,128,64]{2,1,0:T(8,128)S(1)}, f32[8,6,128,64]{2,3,1,0:T(8,128)}, f32[8,6]{1,0:T(8,128)S(1)}, ...), condition=%wide.region_5.5_spmd.clone, body=%wide.region_4.4_spmd.clone.sunk | while | flops 147459 | bytes 2359475 | solution.py:84
  277.8 16.6 %while.128 = (s32[]{:T(128)}, f32[6,128,64]{2,1,0:T(8,128)S(1)}, f32[8,6,128,64]{2,3,1,0:T(8,128)}, f32[8,6]{1,0:T(8,128)S(1)}, f32[8,6,128,64]{2,3,1,0:T(8,128)}, /*index=5*/s32[]{:T(128)}, s32[]{:T(128)}) while((s32[]{:T(128)}, f32[6,128,64]{2,1,0:T(8,128)S(1)}, f32[8,6,128,64]{2,3,1,0:T(8,128)}, f32[8,6]{1,0:T(8,128)S(1)}, ...), condition=%wide.region_5.5_spmd.clone, body=%wide.region_4.4_spmd.clone.sunk | while | flops 147459 | bytes 2359475 | solution.py:84
  328.4 16.5 %psum.105 = f32[2,2048]{1,0:T(2,128)S(1)} all-reduce(f32[2,2048]{1,0:T(2,128)S(1)} %multiply_reduce_fusion.10), channel_id=1, replica_groups=mesh['dp'=8,'tensor'=4] {'tensor'}, use_global_device_ids=true, to_apply=%region_8.9 | all-reduce | flops 4096 | bytes 32768 | tf_op jit(solution)/shard_map/psum | solution.py:198
  354.3 15.5 %psum.106 = f32[2,2048]{1,0:T(2,128)S(1)} all-reduce(f32[2,2048]{1,0:T(2,128)S(1)} %get-tuple-element.1049), channel_id=1, replica_groups=mesh['dp'=8,'tensor'=4] {'tensor'}, use_global_device_ids=true, to_apply=%region_11.12 | all-reduce | flops 4096 | bytes 32768 | tf_op jit(solution)/shard_map/psum | solution.py:223
  378.5 623.6 %while.127 = (s32[]{:T(128)}, f32[2,2048,384]{2,1,0:T(8,128)}, bf16[2,2048,6]{1,2,0:T(8,128)(2,1)}, f32[2,2048,256]{2,1,0:T(8,128)}, bf16[2,2048,384]{2,1,0:T(8,...) while((s32[]{:T(128)}, f32[2,2048,384]{2,1,0:T(8,128)}, ...), condition=%wide.region_32.33_spmd, body=%wide.region_12.32_spmd.sunk | while | flops 16359264256 | bytes 458480448 | solution.py:260
  410.6 71.6 %while.129 = (s32[]{:T(128)}, f32[6,128,64]{2,1,0:T(8,128)}, f32[8,6,128,64]{3,2,1,0:T(8,128)}, f32[8,6,1,1]{1,3,2,0:T(1,128)}, f32[8,6]{1,0:T(8,128)}, /*index=5*/f32[8,6,128,64]{2,3,1,0:T(8,128)}, s32[]{:T(128)}, s32[]{:T(128)}) while((s32[]{:T(128)}, f32[6,128,64]{2,1,0:T(8,128)}, f32[8,6,128,64]{3,2,1,0:T(8,128)}, ...), condition=%wide.region_16.16_spmd.clone, body=%wide.region_15.15_spmd.clone.sunk | while | flops 196611 | bytes 2163904 | solution.py:84
  495.2 11.2 fusion.281
  511.4 54.1 %while.130 = (s32[]{:T(128)}, f32[6,128,64]{2,1,0:T(8,128)S(1)}, f32[8,6]{1,0:T(8,128)S(1)}, f32[8,6,128,64]{3,2,1,0:T(8,128)}, f32[8,6,128,64]{2,3,1,0:T(8,128)...) while((s32[]{:T(128)}, f32[6,128,64]{2,1,0:T(8,128)S(1)}, ...), condition=%wide.region_19.19_spmd.clone, body=%wide.region_17.18_spmd.clone.sunk | while | flops 294910 | bytes 2162984 | solution.py:84
  565.7 13.5 fusion.280
  584.5 11.7 fusion.283
  596.2 12.7 bitcast_add_fusion.9
  608.8 16.9 %fusion.275 = (f32[8,256,6]{1,2,0:T(8,128)S(1)}, f32[8,256,6]{1,2,0:T(8,128)}, f32[8,256,6]{1,2,0:T(8,128)}, f32[8,256,256]{2,1,0:T(8,128)}) fusion(f32[8,256,6]{1,2,0:T(8,128)S(1)} %get-tuple-element.1557, f32[8,256,6]{1,2,0:T(8,128)S(1)} %bitcast.540, f32[8,256,256]{2,1,0:T(8,128)S(1)} %copy-done.27, pred[256,256]{1,0:T(8,128)(4,1)S(1)} %copy-done.49, ...), kind=kOutput, calls=%fused_computation.67.clone.1 | convolution fusion | flops 2462543872 | bytes 9224192 | tf_op jit(solution)/shard_map/while/body/eval_jaxpr/transpose(jvp(ctsh,cshp->cthp))/dot_general | solution.py:72
  658.9 14.9 %reduce-window.68 = f32[8,6,2,128]{3,0,1,2:T(8,128)S(1)} reduce-window(f32[8,6,2,128]{3,0,1,2:T(8,128)S(1)} %copy.583, f32[]{:T(128)} %constant.211.clone.1..sunk.1), window={size=1x1x1x128 pad=0_0x0_0x0_0x0_127}, to_apply=%region_25.25 | reduce-window | flops 1560576 | bytes 98308 | tf_op jit(solution)/shard_map/reduce-window.32
  720.5 71.6 %while.129 = (s32[]{:T(128)}, f32[6,128,64]{2,1,0:T(8,128)}, f32[8,6,128,64]{3,2,1,0:T(8,128)}, f32[8,6,1,1]{1,3,2,0:T(1,128)}, f32[8,6]{1,0:T(8,128)}, /*index=5*/f32[8,6,128,64]{2,3,1,0:T(8,128)}, s32[]{:T(128)}, s32[]{:T(128)}) while((s32[]{:T(128)}, f32[6,128,64]{2,1,0:T(8,128)}, f32[8,6,128,64]{3,2,1,0:T(8,128)}, ...), condition=%wide.region_16.16_spmd.clone, body=%wide.region_15.15_spmd.clone.sunk | while | flops 196611 | bytes 2163904 | solution.py:84
  805.2 11.2 fusion.281
  821.4 54.1 %while.130 = (s32[]{:T(128)}, f32[6,128,64]{2,1,0:T(8,128)S(1)}, f32[8,6]{1,0:T(8,128)S(1)}, f32[8,6,128,64]{3,2,1,0:T(8,128)}, f32[8,6,128,64]{2,3,1,0:T(8,128)...) while((s32[]{:T(128)}, f32[6,128,64]{2,1,0:T(8,128)S(1)}, ...), condition=%wide.region_19.19_spmd.clone, body=%wide.region_17.18_spmd.clone.sunk | while | flops 294910 | bytes 2162984 | solution.py:84
  875.6 13.5 fusion.280
  894.4 11.7 fusion.283
  906.1 12.7 bitcast_add_fusion.9
  918.8 16.9 %fusion.275 = (f32[8,256,6]{1,2,0:T(8,128)S(1)}, f32[8,256,6]{1,2,0:T(8,128)}, f32[8,256,6]{1,2,0:T(8,128)}, f32[8,256,256]{2,1,0:T(8,128)}) fusion(f32[8,256,6]{1,2,0:T(8,128)S(1)} %get-tuple-element.1557, f32[8,256,6]{1,2,0:T(8,128)S(1)} %bitcast.540, f32[8,256,256]{2,1,0:T(8,128)S(1)} %copy-done.27, pred[256,256]{1,0:T(8,128)(4,1)S(1)} %copy-done.49, ...), kind=kOutput, calls=%fused_computation.67.clone.1 | convolution fusion | flops 2462543872 | bytes 9224192 | tf_op jit(solution)/shard_map/while/body/eval_jaxpr/transpose(jvp(ctsh,cshp->cthp))/dot_general | solution.py:72
  968.8 14.9 %reduce-window.68 = f32[8,6,2,128]{3,0,1,2:T(8,128)S(1)} reduce-window(f32[8,6,2,128]{3,0,1,2:T(8,128)S(1)} %copy.583, f32[]{:T(128)} %constant.211.clone.1..sunk.1), window={size=1x1x1x128 pad=0_0x0_0x0_0x0_127}, to_apply=%region_25.25 | reduce-window | flops 1560576 | bytes 98308 | tf_op jit(solution)/shard_map/reduce-window.32
  1002.2 10.9 multiply_reduce_fusion.14
  1024.8 18.6 %multiply_reduce_fusion.7 = (f32[384]{0:T(512)S(1)}, f32[384]{0:T(512)S(1)}, f32[384]{0:T(512)S(1)}, f32[384]{0:T(512)}, f32[384]{0:T(512)S(1)}, /*index=5*/f32[2,2048,384]{2,1,0:T(8,128)}) fusion(f32[2,2048,384]{2,1,0:T(8,128)} %get-tuple-element.1195, f32[2,2048,768]{2,1,0:T(8,128)} %fusion.146, f32[2,2048,384]{2,1,0:T(8,128)} %get-tuple-element.1179, ...), kind=kLoop, calls=%fused_computation.183 | loop fusion | flops 28309632 | bytes 31464960 | tf_op jit(solution)/shard_map/transpose(jvp())/reduce_sum | solution.py:44
  1112.0 20.4 %all-to-all-done = bf16[8,96,1030]{2,1,0:T(8,128)(2,1)S(1)} async-done(((bf16[8,96,1030]{2,1,0:T(8,128)(2,1)}), bf16[8,96,1030]{2,1,0:T(8,128)(2,1)S(1)}, u32[]{:S(2)}, u32[]{:S(2)}) %all-to-all-start) | async-done | bytes 1582112 | tf_op jit(solution)/shard_map/all_to_all | solution.py:24
  1136.7 178.3 %reduce-scatter.6.cloned.1.call-done = f32[2,512,768]{2,1,0:T(8,128)} async-done(((f32[2,2048,768]{2,1,0:T(8,128)}), f32[2,512,768]{2,1,0:T(8,128)}) %reduce-scatter.6.cloned.1.call-update) | async-done | bytes 3145744 | tf_op jit(solution)/shard_map/reduce_scatter | solution.py:312
  1320.2 108.9 %reduce-scatter.4.cloned.1.call-done = bf16[2,512,768]{2,1,0:T(8,128)(2,1)} async-done(((bf16[2,2048,768]{2,1,0:T(8,128)(2,1)}), bf16[2,512,768]{2,1,0:T(8,128)(2,1)}) %reduce-scatter.4.cloned.1.call-update) | async-done | bytes 1572880 | tf_op jit(solution)/shard_map/reduce_scatter | solution.py:204
  1433.3 24.6 %all-reduce.22 = (f32[768]{0:T(1024)S(1)}, f32[4,384]{1,0:T(4,128)}, f32[384]{0:T(512)}, f32[4,256]{1,0:T(4,128)S(1)}, f32[256]{0:T(256)S(1)}, /*index=5*/f32[6]{0:T(128)}, f32[6]{0:T(128)}, f32[6]{0:T(128)}, f32[384]{0:T(512)}) all-reduce(f32[768]{0:T(1024)S(1)} %get-tuple-element.1059, ...), channel_id=1, replica_groups=mesh['dp'=8,'tensor'=4] {'dp'}, use_global_device_ids=true, to_apply=%region_37.38 | all-reduce | flops 4370 | bytes 34960 | tf_op jit(solution)/shard_map/psum | solution.py:350
  1457.9 12.1 all-reduce.23
  (915 shorter events, 758.0 us)
Async XLA Ops:
  7.2 40.1 %all-gather.7.cloned.1.call-start = ((), (), s32[]{:S(2)}) async-start(), calls=%async_computation.6 | async-start | bytes 1327104 | tf_op jit(solution)/shard_map/all_gather | solution.py:143
  7.9 147.4 %all-gather.5.cloned.1.call-start = ((), (), s32[]{:S(2)}) async-start(), calls=%async_computation.5 | async-start | bytes 7864320 | tf_op jit(solution)/shard_map/all_gather | solution.py:141
  11.0 26.0 %copy-start.60 = (bf16[384,96]{0,1:T(8,128)(2,1)S(1)}, bf16[384,96]{0,1:T(8,128)(2,1)}, u32[]{:S(2)}) copy-start(bf16[384,96]{0,1:T(8,128)(2,1)} %param.38) | copy-start | bytes 221188
  14.1 330.8 %all-gather.9.cloned.1.call-start = ((), (), s32[]{:S(2)}) async-start(), calls=%async_computation.8 | async-start | bytes 7864320 | tf_op jit(solution)/shard_map/all_gather | solution.py:214
  14.8 1086.2 %reduce-scatter.8.cloned.1.call-start = ((), (), s32[]{:S(2)}) async-start(), calls=%async_computation.10 | async-start | bytes 5242880 | tf_op jit(solution)/shard_map/reduce_scatter | solution.py:313
  15.5 192.1 %copy-start.76 = (f32[1,256]{1,0:T(1,128)}, f32[1,256]{1,0:T(1,128)S(1)}, u32[]{:S(2)}) copy-start(f32[1,256]{1,0:T(1,128)S(1)} %get-tuple-element.1210) | copy-start | bytes 3076
  15.5 192.1 %copy-start.78 = (f32[1,256]{1,0:T(1,128)}, f32[1,256]{1,0:T(1,128)S(1)}, u32[]{:S(2)}) copy-start(f32[1,256]{1,0:T(1,128)S(1)} %get-tuple-element.1211) | copy-start | bytes 3076
  15.6 192.1 %copy-start.80 = (f32[1,256]{1,0:T(1,128)}, f32[1,256]{1,0:T(1,128)S(1)}, u32[]{:S(2)}) copy-start(f32[1,256]{1,0:T(1,128)S(1)} %get-tuple-element.1212) | copy-start | bytes 3076
  15.6 192.1 %copy-start.82 = (f32[1,256]{1,0:T(1,128)}, f32[1,256]{1,0:T(1,128)S(1)}, u32[]{:S(2)}) copy-start(f32[1,256]{1,0:T(1,128)S(1)} %get-tuple-element.1213) | copy-start | bytes 3076
  15.6 167.2 %copy-start.67 = (f32[384]{0:T(512)}, f32[384]{0:T(512)S(1)}, u32[]{:S(2)}) copy-start(f32[384]{0:T(512)S(1)} %get-tuple-element.1062) | copy-start | bytes 4612
  15.6 167.2 %copy-start.69 = (f32[384]{0:T(512)}, f32[384]{0:T(512)S(1)}, u32[]{:S(2)}) copy-start(f32[384]{0:T(512)S(1)} %get-tuple-element.1063) | copy-start | bytes 4612
  15.6 167.2 %copy-start.71 = (f32[384]{0:T(512)}, f32[384]{0:T(512)S(1)}, u32[]{:S(2)}) copy-start(f32[384]{0:T(512)S(1)} %get-tuple-element.1064) | copy-start | bytes 4612
  15.7 167.2 %copy-start.73 = (f32[384]{0:T(512)}, f32[384]{0:T(512)S(1)}, u32[]{:S(2)}) copy-start(f32[384]{0:T(512)S(1)} %get-tuple-element.1065) | copy-start | bytes 4612
  26.1 186.2 %copy-start.58 = (bf16[768,6,1]{0,1,2:T(8,128)(2,1)}, bf16[768,6,1]{0,1,2:T(8,128)(2,1)S(1)}, u32[]{:S(2)}) copy-start(bf16[768,6,1]{0,1,2:T(8,128)(2,1)S(1)} %reshape.534) | copy-start | bytes 27652
  37.0 165.8 %copy-start.43 = (bf16[768,256]{1,0:T(8,128)(2,1)}, bf16[768,256]{1,0:T(8,128)(2,1)S(1)}, u32[]{:S(2)}) copy-start(bf16[768,256]{1,0:T(8,128)(2,1)S(1)} %all_gather.24) | copy-start | bytes 1179652
  50.5 115.4 %copy-start.51 = (bf16[768,768,1]{1,0,2:T(8,128)(2,1)}, bf16[768,768,1]{1,0,2:T(8,128)(2,1)S(1)}, u32[]{:S(2)}) copy-start(bf16[768,768,1]{1,0,2:T(8,128)(2,1)S(1)} %reshape.532) | copy-start | bytes 3538948
  344.9 24.9 %copy-start.53 = (f32[2,2048]{1,0:T(2,128)}, f32[2,2048]{1,0:T(2,128)S(1)}, u32[]{:S(2)}) copy-start(f32[2,2048]{1,0:T(2,128)S(1)} %get-tuple-element.1207) | copy-start | bytes 49156
  654.9 21.9 %copy-start.96 = (f32[2,6]{1,0:T(2,128)S(1)}, f32[2,6]{1,0:T(2,128)}, u32[]{:S(2)}) copy-start(f32[2,6]{1,0:T(2,128)} %get-tuple-element.1739) | copy-start | bytes 148 | tf_op jit(solution)/shard_map/while
  654.9 22.0 %copy-start.11 = (bf16[2048,128]{1,0:T(8,128)(2,1)S(1)}, bf16[2048,128]{1,0:T(8,128)(2,1)}, u32[]{:S(2)}) copy-start(bf16[2048,128]{1,0:T(8,128)(2,1)} %copy-done.9) | copy-start | bytes 1572868 | tf_op jit(solution)/shard_map/while
  654.9 22.0 %copy-start.16 = (f32[8,256,256]{2,1,0:T(8,128)S(1)}, f32[8,256,256]{2,1,0:T(8,128)}, u32[]{:S(2)}) copy-start(f32[8,256,256]{2,1,0:T(8,128)} %get-tuple-element.1564) | copy-start | bytes 6291460 | tf_op jit(solution)/shard_map/while
  964.8 22.0 %copy-start.11 = (bf16[2048,128]{1,0:T(8,128)(2,1)S(1)}, bf16[2048,128]{1,0:T(8,128)(2,1)}, u32[]{:S(2)}) copy-start(bf16[2048,128]{1,0:T(8,128)(2,1)} %copy-done.9) | copy-start | bytes 1572868 | tf_op jit(solution)/shard_map/while
  964.9 22.0 %copy-start.16 = (f32[8,256,256]{2,1,0:T(8,128)S(1)}, f32[8,256,256]{2,1,0:T(8,128)}, u32[]{:S(2)}) copy-start(f32[8,256,256]{2,1,0:T(8,128)} %get-tuple-element.1564) | copy-start | bytes 6291460 | tf_op jit(solution)/shard_map/while
  1024.7 290.3 %reduce-scatter.6.cloned.1.call-start = ((), (), s32[]{:S(2)}) async-start(), calls=%async_computation.9 | async-start | bytes 15728640 | tf_op jit(solution)/shard_map/reduce_scatter | solution.py:312
  1064.5 364.6 %reduce-scatter.4.cloned.1.call-start = ((), (), s32[]{:S(2)}) async-start(), calls=%async_computation.7 | async-start | bytes 7864320 | tf_op jit(solution)/shard_map/reduce_scatter | solution.py:204
  1083.1 21.2 %all-to-all-start.1 = ((bf16[8,384,96]{1,2,0:T(8,128)(2,1)}), bf16[8,384,96]{1,2,0:T(8,128)(2,1)S(1)}, u32[]{:S(2)}, u32[]{:S(2)}) async-start(bf16[8,384,96]{1,2,0:T(8,128)(2,1)} %bitcast.86), calls=%async_computation.4 | async-start | bytes 1179648 | tf_op jit(solution)/shard_map/all_to_all | solution.py:24
  1105.1 27.3 %all-to-all-start = ((bf16[8,96,1030]{2,1,0:T(8,128)(2,1)}), bf16[8,96,1030]{2,1,0:T(8,128)(2,1)S(1)}, u32[]{:S(2)}, u32[]{:S(2)}) async-start(bf16[8,96,1030]{2,1,0:T(8,128)(2,1)} %pad_maximum_fusion.3), calls=%async_computation.3 | async-start | bytes 3538944 | tf_op jit(solution)/shard_map/all_to_all | solution.py:24
  1109.3 205.7 %copy-start.30 = (bf16[2,512,768]{2,1,0:T(8,128)(2,1)S(1)}, bf16[2,512,768]{2,1,0:T(8,128)(2,1)}, u32[]{:S(2)}) copy-start(bf16[2,512,768]{2,1,0:T(8,128)(2,1)} %param.25) | copy-start | bytes 4718596
  1109.3 205.7 %copy-start.62 = (f32[2,512]{1,0:T(2,128)S(1)}, f32[2,512]{1,0:T(2,128)}, u32[]{:S(2)}) copy-start(f32[2,512]{1,0:T(2,128)} %copy-done.61) | copy-start | bytes 12292
  1109.4 205.7 %copy-start.66 = (f32[768]{0:T(1024)S(1)}, f32[768]{0:T(1024)}, u32[]{:S(2)}) copy-start(f32[768]{0:T(1024)} %param.26) | copy-start | bytes 9220
  1109.4 360.6 %all-reduce.26.cloned.1.call-start = ((), (), s32[]{:S(2)}) async-start(), calls=%async_computation.11 | async-start | bytes 196608 | tf_op jit(solution)/shard_map/psum | solution.py:364
  1136.7 292.4 %copy-start.38 = (bf16[2,512,768]{2,1,0:T(8,128)(2,1)S(1)}, bf16[2,512,768]{2,1,0:T(8,128)(2,1)}, u32[]{:S(2)}) copy-start(bf16[2,512,768]{2,1,0:T(8,128)(2,1)} %param.39) | copy-start | bytes 4718596
  1136.7 292.4 %copy-start.75 = (f32[2,512]{1,0:T(2,128)S(1)}, f32[2,512]{1,0:T(2,128)}, u32[]{:S(2)}) copy-start(f32[2,512]{1,0:T(2,128)} %get-tuple-element.1208) | copy-start | bytes 12292
  (141 other events, 866.9 us)
Sparse Core Ops, SparseCore 0:
  9.9 27.8 all-gather.6
  39.9 115.3 all-gather.4
  156.9 113.5 all-gather.8
  1024.9 75.3 reduce-scatter.7
  1102.6 212.3 reduce-scatter.5
  1317.3 111.7 reduce-scatter.3
  1432.1 34.8 all-reduce.25
where the time goes:
time: 1490 us; the launch traced here: 1480 us
  waiting for transfers between devices  414 us (28%)
  local copies, waits for them, and re-layouts  369 us (25%)
  other arithmetic  285 us (19%)
  matrix products  280 us (19%)
  blocking collectives  100 us (7%)
  between operations  15.1 us (1%)
    reduce_scatter x1, waiting for transfers between devices, local(): lax.psum_scatter(normed_grad, 'tensor', scatter_dimension=1, tiled=True)  178 us
    dynamic_slice x96, local copies, waits for them, and re-layouts, scan_heads(): lax.scan(advance, initial, (block_decay, fresh_states))  128 us
    reduce_scatter x1, waiting for transfers between devices, local(): lax.psum_scatter(partial_output_rows.astype(jnp.bfloat16), 'tensor', scat...  109 us
    all_gather x1, waiting for transfers between devices, local(): lax.all_gather(normalized_local_rows, 'tensor', axis=1, tiled=True)  105 us
    dot_general x8, matrix products, scan_heads(): jnp.einsum('ctsh,cshp->cthp', scores, blocked_x, precision=TOP_PRECISION)  103 us
    another operation x35, other arithmetic  49.7 us
    dot_general x8, matrix products, scan_heads(): jnp.einsum('csn,csh,cshp->chnp', blocked_b, to_end, blocked_x, precision=...  48 us
    dynamic_update_slice x32, other arithmetic, scan_heads(): lax.scan(advance, initial, (block_decay, fresh_states))  39.4 us
  transfers between devices with their start and end apart: 9, of which 4 were waited for; matrix products, arithmetic and copies ran while one was open for 18% of the time, Pallas kernels for 0%

commit v1 on v0

v1 whole, which is shorter than its diff:
```python
import functools

import jax
import jax.numpy as jnp
from jax import lax
from jax.experimental import pallas as pl
from jax.experimental.pallas import tpu as pltpu
from jax.sharding import PartitionSpec as P

P_SIZE = 64
SPAN = 256
HALF = SPAN // 2
EPSILON = 1e-05
LOG2E = 1.4426950408889634
F32 = jnp.float32
BF16 = jnp.bfloat16
VMEM_LIMIT = 60 * 1024 * 1024
WIDE = 512


def dot(a, b):
    return jnp.dot(a, b, preferred_element_type=F32)


def dot_nt(a, b):
    return lax.dot_general(a, b, (((1,), (1,)), ((), ())), preferred_element_type=F32)


def dot_tn(a, b):
    return lax.dot_general(a, b, (((0,), (0,)), ((), ())), preferred_element_type=F32)


def sigmoid(v):
    return 0.5 * jnp.tanh(0.5 * v) + 0.5


def split2(v):
    hi = v.astype(BF16)
    return hi, (v - hi.astype(F32)).astype(BF16)


def lanes_of(shape):
    return lax.broadcasted_iota(jnp.int32, shape, len(shape) - 1)


def packed(v, heads):
    v = jnp.where(lanes_of(v.shape) < heads, v, 0.0)
    hi = v.astype(BF16).astype(F32)
    low = (v - hi).astype(BF16).astype(F32)
    return (hi + pltpu.roll(low, 32, 1)).astype(BF16)


def spread_heads(pk, sel):
    return dot(pk, sel)


def gather_heads(v, selt):
    hi, low = split2(v)
    return dot(hi, selt) + dot(low, selt)


def cumulate(tri, v, heads):
    v = jnp.where(lanes_of(v.shape) < heads, v, 0.0)
    p0 = v.astype(BF16).astype(F32)
    r = v - p0
    p1 = r.astype(BF16).astype(F32)
    p2 = r - p1
    pk = (p0 + pltpu.roll(p1, 32, 1) + pltpu.roll(p2, 64, 1)).astype(BF16)
    s = dot(tri, pk)
    n = s.shape[1]
    s = s + pltpu.roll(s, n - 32, 1) + pltpu.roll(s, n - 64, 1)
    return jnp.where(lanes_of(v.shape) < heads, s, 0.0)


def block_rows(b, size):
    return pl.ds(pl.multiple_of(b * size, size), size)


def front_kernel(
    heads,
    x_ref, xh_ref, gain_ref, wi_ref, wsd_ref, ti_ref, ts_ref, dpar_ref, sel_ref, tri_ref,
    h_ref, rawi_ref, raws_ref, xs_ref, bc_ref, draw_ref, acs_ref, bs_ref, fresh_ref, dec_ref,
    hh_ref, w_ref,
):
    seqs, ext, di = rawi_ref.shape
    span = ext - 16
    per = span // SPAN
    state = bc_ref.shape[1] // 2
    sh = raws_ref.shape[2]

    def norm(v):
        v = v.astype(F32)
        return (v * lax.rsqrt(jnp.mean(v * v, axis=-1, keepdims=True) + EPSILON) * gain_ref[...]).astype(BF16)

    hh_ref[...] = norm(xh_ref[...])
    for s in range(seqs):
        rawi_ref[s, 0:16, :] = dot(hh_ref[16 * s : 16 * s + 16, :], wi_ref[...])
        raws_ref[s, 0:16, :] = dot(hh_ref[16 * s : 16 * s + 16, :], wsd_ref[:, :sh])

    def seq_step(s, carry):
        def norm_step(b, c):
            rows = block_rows(s * per + b, SPAN)
            h_ref[rows, :] = norm(x_ref[rows, :])
            return c

        lax.fori_loop(0, per, norm_step, 0)
        rows = block_rows(s, span)
        for c0 in range(0, di, WIDE):
            rawi_ref[s, 16:ext, c0 : c0 + WIDE] = dot(h_ref[rows, :], wi_ref[:, c0 : c0 + WIDE])
        sd = dot(h_ref[rows, :], wsd_ref[...])
        raws_ref[s, 16:ext, :] = sd[:, :sh]
        draw_ref[rows, :] = sd[:, sh:] + dpar_ref[0:1, :]

        def conv(raw, par, out, cols):
            def step(r, c):
                r0 = pl.multiple_of(r * 128, 128)
                v = raw[s, pl.ds(r0, 144), cols]
                acc = par[4:5, cols] + par[0:1, cols] * v[13:141]
                for k in range(1, 4):
                    acc = acc + par[k : k + 1, cols] * v[13 + k : 141 + k]
                out[pl.ds(pl.multiple_of(s * span + r0, 128), 128), cols] = (acc * sigmoid(acc)).astype(BF16)
                return c

            lax.fori_loop(0, span // 128, step, 0)

        for c0 in range(0, di, 256):
            conv(rawi_ref, ti_ref, xs_ref, slice(c0, c0 + 256))
        for c0 in range(0, sh, 256):
            conv(raws_ref, ts_ref, bc_ref, slice(c0, c0 + 256))

        def block_step(j, c):
            b = s * per + j
            rows = block_rows(b, SPAN)
            x = draw_ref[rows, :]
            e = jnp.log1p(jnp.exp(-jnp.abs(x)))
            dt = jnp.maximum(x, 0.0) + e
            lg = jnp.where(x < -20.0, x * LOG2E, jnp.log2(jnp.maximum(dt, 1e-30)))
            acs = cumulate(tri_ref[...], dt * dpar_ref[1:2, :], heads)
            bs = acs - lg
            acs_ref[rows, :] = acs
            bs_ref[rows, :] = bs
            end = acs[SPAN - 1 : SPAN, :]
            w_ref[...] = packed(jnp.exp2(end - bs), heads)
            bt = bc_ref[rows, :state].astype(F32).T.astype(BF16)
            dk = packed(jnp.broadcast_to(jnp.exp2(end), (8, 128)), heads)
            for c0 in range(0, di, WIDE):
                cols = slice(c0, c0 + WIDE)
                w = spread_heads(w_ref[...], sel_ref[:, cols])
                wx = (w * xs_ref[rows, cols].astype(F32)).astype(BF16)
                fresh_ref[b, :, cols] = dot(bt, wx)
                dec_ref[b, :, cols] = spread_heads(dk, sel_ref[:, cols])
            return c

        lax.fori_loop(0, per, block_step, 0)
        return carry

    lax.fori_loop(0, seqs, seq_step, 0)


def mid_kernel(
    heads,
    x_ref, c_ref, h_ref, wg_ref, wo_ref, ggain_ref, skip_ref, xs_ref, bc_ref, acs_ref, bs_ref,
    sin_ref, fresh_ref, dec_ref, sel_ref, selt_ref,
    out_ref, yn_ref, dgate_ref, dy_ref, rr_ref, vv_ref, gg_ref, sk_ref, go_ref,
    y_ref, gate_ref, q_ref, g_ref, acst_ref, bst_ref, ea_ref,
):
    tokens, di = xs_ref.shape
    seqs = sin_ref.shape[0]
    blocks = tokens // SPAN
    per = blocks // seqs
    state = bc_ref.shape[1] // 2
    lower = lax.broadcasted_iota(jnp.int32, (HALF, HALF), 0) >= lax.broadcasted_iota(jnp.int32, (HALF, HALF), 1)
    first = lanes_of((HALF, 128)) < P_SIZE
    gg_ref[...] = jnp.zeros_like(gg_ref)
    sk_ref[...] = jnp.zeros_like(sk_ref)

    def block_step(b, carry):
        rows = block_rows(b, SPAN)
        s = b // per
        j = b - s * per
        acst_ref[...] = acs_ref[rows, :].T
        bst_ref[...] = bs_ref[rows, :].T
        ea_ref[...] = packed(jnp.exp2(acs_ref[rows, :]), heads)
        bb = bc_ref[rows, :state]
        cc = bc_ref[rows, state:]
        g00 = dot_nt(cc[:HALF], bb[:HALF])
        g10 = dot_nt(cc[HALF:], bb[:HALF])
        g11 = dot_nt(cc[HALF:], bb[HALF:])
        for p in range(di // 128):
            cols = slice(128 * p, 128 * p + 128)
            xp = xs_ref[rows, cols]
            y0, y1 = [], []
            for h in (2 * p, 2 * p + 1):
                a0 = acs_ref[block_rows(2 * b, HALF), h : h + 1]
                a1 = acs_ref[block_rows(2 * b + 1, HALF), h : h + 1]
                r0 = bst_ref[h : h + 1, :HALF]
                r1 = bst_ref[h : h + 1, HALF:]
                m00 = jnp.where(lower, jnp.exp2(a0 - r0) * g00, 0.0).astype(BF16)
                m10 = (jnp.exp2(a1 - r0) * g10).astype(BF16)
                m11 = jnp.where(lower, jnp.exp2(a1 - r1) * g11, 0.0).astype(BF16)
                y0.append(dot(m00, xp[:HALF]))
                y1.append(dot(jnp.concatenate([m10, m11], axis=1), xp))
            y_ref[0:HALF, cols] = jnp.where(first, y0[0], y0[1])
            y_ref[HALF:SPAN, cols] = jnp.where(first, y1[0], y1[1])

        ss = jnp.zeros((SPAN, 1), F32)
        for c0 in range(0, di, WIDE):
            cols = slice(c0, c0 + WIDE)
            prev = sin_ref[s, :, cols].astype(F32)
            later = dec_ref[s * per, 0:1, cols] * prev + fresh_ref[s * per, :, cols]
            s_in = jnp.where(j == 0, prev, later).astype(BF16)
            ea = spread_heads(ea_ref[...], sel_ref[:, cols])
            ynos = y_ref[:, cols] + ea * dot(cc, s_in)
            y_ref[:, cols] = ynos
            y = ynos + skip_ref[0:1, cols] * xs_ref[rows, cols].astype(F32)
            gate = dot(h_ref[rows, :], wg_ref[:, cols])
            gate_ref[:, cols] = gate
            g = y * (gate * sigmoid(gate))
            g_ref[:, cols] = g
            ss = ss + jnp.sum(g * g, axis=-1, keepdims=True)
        r2 = lax.rsqrt(ss / di + EPSILON)
        qg = jnp.zeros((SPAN, 1), F32)
        for c0 in range(0, di, WIDE):
            cols = slice(c0, c0 + WIDE)
            g = g_ref[:, cols]
            gain = ggain_ref[0:1, cols]
            yn_ref[rows, cols] = (g * r2 * gain).astype(BF16)
            dyn = dot(c_ref[rows, :], wo_ref[:, cols])
            gg_ref[0:1, cols] += jnp.sum(dyn * (g * r2), axis=0, keepdims=True)
            q = dyn * gain
            q_ref[:, cols] = q
            qg = qg + jnp.sum(q * g, axis=-1, keepdims=True)
        out_ref[rows, :] = (x_ref[rows, :].astype(F32) + dot_nt(yn_ref[rows, :], wo_ref[...])).astype(BF16)
        coef = r2 * r2 * r2 * (qg / di)
        rr = jnp.zeros((SPAN, 128), F32)
        dk = jnp.zeros((SPAN, 128), F32)
        ct = cc.astype(F32).T.astype(BF16)
        for c0 in range(0, di, WIDE):
            cols = slice(c0, c0 + WIDE)
            xf = xs_ref[rows, cols].astype(F32)
            ynos = y_ref[:, cols]
            y = ynos + skip_ref[0:1, cols] * xf
            gate = gate_ref[:, cols]
            sg = sigmoid(gate)
            dg = r2 * q_ref[:, cols] - coef * g_ref[:, cols]
            dgate_ref[rows, cols] = (dg * y * (sg * (1.0 + gate * (1.0 - sg)))).astype(BF16)
            dyb = (dg * (gate * sg)).astype(BF16)
            dy_ref[rows, cols] = dyb
            dy = dyb.astype(F32)
            rr = rr + gather_heads(dy * ynos, selt_ref[cols, :])
            dk = dk + gather_heads(dy * xf, selt_ref[cols, :])
            ea = spread_heads(ea_ref[...], sel_ref[:, cols])
            vv_ref[b, :, cols] = dot(ct, (ea * dy).astype(BF16))
        rr_ref[rows, :] = rr
        sk_ref[0:1, :] += jnp.sum(dk, axis=0, keepdims=True)
        return carry

    lax.fori_loop(0, blocks, block_step, 0)
    for c0 in range(0, di, WIDE):
        cols = slice(c0, c0 + WIDE)
        go_ref[:, cols] = dot_tn(c_ref[...], yn_ref[:, cols]).astype(BF16)


def back_kernel(
    heads,
    xs_ref, bc_ref, draw_ref, acs_ref, bs_ref, sin_ref, fresh_ref, dec_ref, ds_ref, vv_ref, dy_ref, rr_ref,
    rawi_ref, raws_ref, ti_ref, ts_ref, dpar_ref, skip_ref, sel_ref, selt_ref, tri_ref, triu_ref,
    dpi_ref, dps_ref, dd_ref, small_ref, tgi_ref, tgs_ref,
    acst_ref, ea_ref, w_ref, dg_ref, dx_ref, dbc_ref,
):
    tokens, di = xs_ref.shape
    seqs, ext, _ = rawi_ref.shape
    span = ext - 16
    blocks = tokens // SPAN
    per = blocks // seqs
    state = bc_ref.shape[1] // 2
    sh = 2 * state
    upper = lax.broadcasted_iota(jnp.int32, (HALF, HALF), 0) <= lax.broadcasted_iota(jnp.int32, (HALF, HALF), 1)
    first = lanes_of((HALF, 128)) < P_SIZE
    first_all = lanes_of((SPAN, 128)) < P_SIZE
    small_ref[...] = jnp.zeros_like(small_ref)
    tgi_ref[...] = jnp.zeros_like(tgi_ref)
    tgs_ref[...] = jnp.zeros_like(tgs_ref)

    def block_step(b, carry):
        rows = block_rows(b, SPAN)
        s = b // per
        j = b - s * per
        acst_ref[...] = acs_ref[rows, :].T
        acs = acs_ref[rows, :]
        bs = bs_ref[rows, :]
        end = acs[SPAN - 1 : SPAN, :]
        ea_ref[...] = packed(jnp.exp2(acs), heads)
        w_ref[...] = packed(jnp.exp2(end - bs), heads)
        bb = bc_ref[rows, :state]
        cc = bc_ref[rows, state:]
        g00 = dot_nt(bb[:HALF], cc[:HALF])
        g01 = dot_nt(bb[:HALF], cc[HALF:])
        g11 = dot_nt(bb[HALF:], cc[HALF:])
        dg_ref[...] = jnp.zeros_like(dg_ref)
        for p in range(di // 128):
            cols = slice(128 * p, 128 * p + 128)
            xp = xs_ref[rows, cols]
            dyp = dy_ref[rows, cols]
            d0, d1 = [], []
            for i, h in enumerate((2 * p, 2 * p + 1)):
                keep = first_all if i == 0 else jnp.logical_not(first_all)
                xm = jnp.where(keep, xp, jnp.zeros_like(xp))
                b0 = bs_ref[block_rows(2 * b, HALF), h : h + 1]
                b1 = bs_ref[block_rows(2 * b + 1, HALF), h : h + 1]
                r0 = acst_ref[h : h + 1, :HALF]
                r1 = acst_ref[h : h + 1, HALF:]
                e00 = jnp.where(upper, jnp.exp2(r0 - b0), 0.0)
                e01 = jnp.exp2(r1 - b0)
                e11 = jnp.where(upper, jnp.exp2(r1 - b1), 0.0)
                m0 = jnp.concatenate([(e00 * g00).astype(BF16), (e01 * g01).astype(BF16)], axis=1)
                m1 = (e11 * g11).astype(BF16)
                d0.append(dot(m0, dyp))
                d1.append(dot(m1, dyp[HALF:]))
                dm0 = dot_nt(xm[:HALF], dyp)
                dm1 = dot_nt(xm[HALF:], dyp[HALF:])
                dg_ref[0] += dm0[:, :HALF] * e00
                dg_ref[1] += dm0[:, HALF:] * e01
                dg_ref[2] += dm1 * e11
            dx_ref[0:HALF, cols] = jnp.where(first, d0[0], d0[1])
            dx_ref[HALF:SPAN, cols] = jnp.where(first, d1[0], d1[1])

        dg00 = dg_ref[0]
        dg01 = dg_ref[1]
        dg11 = dg_ref[2]
        db0 = dot(jnp.concatenate([dg00, dg01], axis=1).astype(BF16), cc)
        db1 = dot(dg11.astype(BF16), cc[HALF:])
        dc0 = dot(dg00.T.astype(BF16), bb[:HALF])
        dc1 = dot(jnp.concatenate([dg01.T, dg11.T], axis=1).astype(BF16), bb)
        db = jnp.concatenate([db0, db1], axis=0)
        dc = jnp.concatenate([dc0, dc1], axis=0)
        rr = rr_ref[rows, :]
        pin = jnp.zeros((SPAN, 128), F32)
        pst = jnp.zeros((SPAN, 128), F32)
        endsum = jnp.zeros((8, 128), F32)
        for c0 in range(0, di, WIDE):
            cols = slice(c0, c0 + WIDE)
            prev = sin_ref[s, :, cols].astype(F32)
            later = dec_ref[s * per, 0:1, cols] * prev + fresh_ref[s * per, :, cols]
            s_in = jnp.where(j == 0, prev, later).astype(BF16)
            dlast = ds_ref[s, :, cols].astype(F32)
            dprev = dec_ref[s * per + per - 1, 0:1, cols] * dlast + vv_ref[s * per + per - 1, :, cols]
            ds = jnp.where(j == per - 1, dlast, dprev).astype(BF16)
            w = spread_heads(w_ref[...], sel_ref[:, cols])
            ea = spread_heads(ea_ref[...], sel_ref[:, cols])
            xf = xs_ref[rows, cols].astype(F32)
            dyf = dy_ref[rows, cols].astype(F32)
            dxs = w * dot(bb, ds)
            dxi = dx_ref[:, cols]
            pin = pin + gather_heads(dxi * xf, selt_ref[cols, :])
            pst = pst + gather_heads(dxs * xf, selt_ref[cols, :])
            both = jnp.sum(ds.astype(F32) * s_in.astype(F32), axis=0, keepdims=True) * dec_ref[b, 0:1, cols]
            endsum = endsum + gather_heads(jnp.broadcast_to(both, (8, WIDE)), selt_ref[cols, :])
            dc = dc + dot_nt((ea * dyf).astype(BF16), s_in)
            db = db + dot_nt((w * xf).astype(BF16), ds)
            dx_ref[:, cols] = dxi + dxs + skip_ref[0:1, cols] * dyf
        dbc_ref[:, :state] = db
        dbc_ref[:, state:] = dc
        pp = pin + pst
        da = cumulate(triu_ref[...], rr - pp, heads) + (endsum[0:1, :] + jnp.sum(pst, axis=0, keepdims=True))
        x = draw_ref[rows, :]
        sg = 1.0 / (1.0 + jnp.exp(-x))
        dt = jnp.maximum(x, 0.0) + jnp.log1p(jnp.exp(-jnp.abs(x)))
        ratio = jnp.where(x < -20.0, 1.0, sg / jnp.maximum(dt, 1e-30))
        ak = dpar_ref[2:3, :]
        dd = da * ak * sg + pp * ratio
        dd_ref[rows, :] = dd.astype(BF16)
        small_ref[0:1, :] += jnp.sum(da * dt * ak, axis=0, keepdims=True)
        small_ref[1:2, :] += jnp.sum(dd, axis=0, keepdims=True)

        def conv_back(raw, par, dact, dpre, tg, cols):
            def step(r, c):
                r0 = pl.multiple_of(r * HALF, HALF)
                v = raw[s, pl.ds(pl.multiple_of(j * SPAN + r0, HALF), HALF + 16), cols]
                sh_v = [v[13 + k : 13 + k + HALF] for k in range(4)]
                pre = par[4:5, cols] + par[0:1, cols] * sh_v[0]
                for k in range(1, 4):
                    pre = pre + par[k : k + 1, cols] * sh_v[k]
                sg = sigmoid(pre)
                dp = dact[pl.ds(r0, HALF), cols] * (sg * (1.0 + pre * (1.0 - sg)))
                dpre[pl.ds(pl.multiple_of(b * SPAN + r0, HALF), HALF), cols] = dp
                for k in range(4):
                    tg[k : k + 1, cols] += jnp.sum(dp * sh_v[k], axis=0, keepdims=True)
                tg[4:5, cols] += jnp.sum(dp, axis=0, keepdims=True)
                return c

            lax.fori_loop(0, SPAN // HALF, step, 0)

        for c0 in range(0, di, 256):
            conv_back(rawi_ref, ti_ref, dx_ref, dpi_ref, tgi_ref, slice(c0, c0 + 256))
        for c0 in range(0, sh, 256):
            conv_back(raws_ref, ts_ref, dbc_ref, dps_ref, tgs_ref, slice(c0, c0 + 256))
        return carry

    lax.fori_loop(0, blocks, block_step, 0)


def last_kernel(
    x_ref, c_ref, gain_ref, h_ref, dpi_ref, dps_ref, hi_ref, hs_ref, dd_ref, dgate_ref, ti_ref, ts_ref,
    wi_ref, wg_ref, wsd_ref,
    ig_ref, gi_ref, gg_ref, gsd_ref, ng_ref,
    din_ref, dsd_ref,
):
    tokens, di = dgate_ref.shape
    seqs = hi_ref.shape[0]
    span = tokens // seqs
    sh = dps_ref.shape[1]
    ng_ref[...] = jnp.zeros_like(ng_ref)
    dsd_ref[:, sh:] = dd_ref[...]

    def conv_t(dpre, halo, par, out, cols):
        for s in range(seqs):
            for r0 in range(0, span, HALF):
                base = s * span + r0
                v = dpre[base : base + HALF, cols]
                if r0 + HALF < span:
                    nxt = dpre[base + HALF : base + HALF + 8, cols]
                else:
                    nxt = halo[s, :, cols]
                v = jnp.concatenate([v, nxt], axis=0)
                acc = par[3:4, cols] * v[0:HALF]
                for k in range(3):
                    acc = acc + par[k : k + 1, cols] * v[3 - k : 3 - k + HALF]
                out[base : base + HALF, cols] = acc.astype(BF16)

    for c0 in range(0, di, 256):
        conv_t(dpi_ref, hi_ref, ti_ref, din_ref, slice(c0, c0 + 256))
    for c0 in range(0, sh, 256):
        conv_t(dps_ref, hs_ref, ts_ref, dsd_ref, slice(c0, c0 + 256))

    for c0 in range(0, di, WIDE):
        cols = slice(c0, c0 + WIDE)
        gi_ref[:, cols] = dot_tn(h_ref[...], din_ref[:, cols]).astype(BF16)
        gg_ref[:, cols] = dot_tn(h_ref[...], dgate_ref[:, cols]).astype(BF16)
    gsd_ref[...] = dot_tn(h_ref[...], dsd_ref[...]).astype(BF16)

    def step(b, carry):
        rows = block_rows(b, SPAN)
        dh = dot_nt(dgate_ref[rows, :], wg_ref[...])
        dh = dh + dot_nt(din_ref[rows, :], wi_ref[...])
        dh = dh + dot_nt(dsd_ref[rows, :], wsd_ref[...])
        u = x_ref[rows, :].astype(F32)
        r1 = lax.rsqrt(jnp.mean(u * u, axis=-1, keepdims=True) + EPSILON)
        ng_ref[0:1, :] += jnp.sum(dh * u * r1, axis=0, keepdims=True)
        e = dh * gain_ref[...]
        m = jnp.mean(e * u, axis=-1, keepdims=True)
        ig_ref[rows, :] = (c_ref[rows, :].astype(F32) + r1 * e - u * (r1 * r1 * r1 * m)).astype(BF16)
        return carry

    lax.fori_loop(0, tokens // SPAN, step, 0)


def call(kernel, outs, scratch, *args, name):
    return pl.pallas_call(
        kernel,
        out_shape=[jax.ShapeDtypeStruct(s, d) for s, d in outs],
        in_specs=[pl.BlockSpec(memory_space=pltpu.VMEM)] * len(args),
        out_specs=[pl.BlockSpec(memory_space=pltpu.VMEM)] * len(outs),
        scratch_shapes=[pltpu.VMEM(s, d) for s, d in scratch],
        compiler_params=pltpu.CompilerParams(vmem_limit_bytes=VMEM_LIMIT),
        name=name,
    )(*args)


def shifted(v, axis, by):
    n = lax.axis_size(axis)
    return lax.ppermute(v, axis, [(i, i + by) for i in range(n) if 0 <= i + by < n])


def local(
    block_input, norm_gain, input_gate_inner_weight, input_shared_weight, input_delta_weight, conv_inner, shift_inner,
    conv_shared, shift_shared, decay_log, delta_bias, skip_gain, gated_gain, output_projection_weight, cotangent,
):
    nt = lax.axis_size("tensor")
    nd = lax.axis_size("dp")
    both = ("tensor", "dp")
    me = lax.axis_index("tensor")
    seqs, span, dim = block_input.shape
    tokens = seqs * span
    blocks = tokens // SPAN
    rows, _, dcol = input_gate_inner_weight.shape
    di = dcol * nt
    sh = input_shared_weight.shape[1]
    state = sh // 2
    hloc = input_delta_weight.shape[1]
    heads = hloc * nt

    delta_w = lax.dynamic_update_slice(jnp.zeros((rows, 128), BF16), input_delta_weight, (0, me * hloc))
    pack = jnp.concatenate(
        [input_gate_inner_weight[:, 1], input_gate_inner_weight[:, 0], output_projection_weight.T, delta_w], axis=1
    )
    full = lax.all_gather(pack, both, axis=0).reshape(nt, dim, 3 * dcol + 128)
    wi, wg, wo = (full[:, :, dcol * k : dcol * (k + 1)].transpose(1, 0, 2).reshape(dim, di) for k in range(3))
    wd = jnp.sum(full[:, :, 3 * dcol :].astype(F32), axis=0).astype(BF16)
    ws = lax.all_gather(input_shared_weight, "dp", axis=0, tiled=True)
    wsd = jnp.concatenate([ws, wd], axis=1)
    chan = jnp.concatenate([conv_inner.astype(F32), shift_inner.astype(F32)[None], gated_gain[None]], axis=0)
    head = jnp.stack([decay_log, delta_bias, skip_gain])
    par = jnp.concatenate([chan, jnp.pad(head, ((0, 3), (0, dcol - hloc)))], axis=0)
    par = lax.all_gather(par, "tensor", axis=0)
    chan = par[:, :6].transpose(1, 0, 2).reshape(6, di)
    head = par[:, 6:9, :hloc].transpose(1, 0, 2).reshape(3, heads)
    ti = jnp.pad(chan[:5], ((0, 3), (0, 0)))
    ts = jnp.pad(jnp.concatenate([conv_shared.astype(F32), shift_shared.astype(F32)[None]], axis=0), ((0, 3), (0, 0)))
    ak = -jnp.exp(head[0])
    dpar = jnp.pad(jnp.stack([head[1], ak * LOG2E, ak]), ((0, 5), (0, 128 - heads)))
    ggain = chan[5:6]
    skip = jnp.repeat(head[2], P_SIZE)[None]
    gain = norm_gain[None]

    lane = jnp.arange(128)
    owner = jnp.arange(di) // P_SIZE
    sel = ((lane[:, None] % 32 == owner[None]) & (lane[:, None] < 64)).astype(BF16)
    selt = (lane[None] == owner[:, None]).astype(BF16)
    at = jnp.arange(SPAN)
    tri = (at[:, None] >= at[None]).astype(BF16)
    triu = tri.T

    x = block_input.reshape(tokens, dim)
    c = cotangent.reshape(tokens, dim)
    xh = shifted(block_input[:, span - 16 :], "tensor", 1).reshape(seqs * 16, dim)

    h, rawi, raws, xs, bc, draw, acs, bs, fresh, dec = call(
        functools.partial(front_kernel, heads),
        [((tokens, dim), BF16), ((seqs, span + 16, di), F32), ((seqs, span + 16, sh), F32), ((tokens, di), BF16),
         ((tokens, sh), BF16), ((tokens, 128), F32), ((tokens, 128), F32), ((tokens, 128), F32),
         ((blocks, state, di), F32), ((blocks, 8, di), F32)],
        [((seqs * 16, dim), BF16), ((SPAN, 128), BF16)],
        x, xh, gain, wi, wsd, ti, ts, dpar, sel, tri, name="front",
    )

    fr = fresh.reshape(seqs, blocks // seqs, state, di)
    de = dec.reshape(seqs, blocks // seqs, 8, di)[:, :, 0:1]
    whole, mine = de[:, 0], fr[:, 0]
    for j in range(1, blocks // seqs):
        mine = de[:, j] * mine + fr[:, j]
        whole = de[:, j] * whole
    sin = jnp.zeros((seqs, state, di), BF16)
    for _ in range(nt - 1):
        sin = shifted((mine + whole * sin.astype(F32)).astype(BF16), "tensor", 1)

    out, yn, dgate, dy, rr, vv, ggg, skg, go = call(
        functools.partial(mid_kernel, heads),
        [((tokens, dim), BF16), ((tokens, di), BF16), ((tokens, di), BF16), ((tokens, di), BF16), ((tokens, 128), F32),
         ((blocks, state, di), F32), ((8, di), F32), ((8, 128), F32), ((dim, di), BF16)],
        [((SPAN, di), F32)] * 4 + [((128, SPAN), F32)] * 2 + [((SPAN, 128), BF16)],
        x, c, h, wg, wo, ggain, skip, xs, bc, acs, bs, sin, fresh, dec, sel, selt, name="mid",
    )

    vr = vv.reshape(seqs, blocks // seqs, state, di)
    mine = vr[:, blocks // seqs - 1]
    for j in range(blocks // seqs - 2, -1, -1):
        mine = de[:, j] * mine + vr[:, j]
    ds = jnp.zeros((seqs, state, di), BF16)
    for _ in range(nt - 1):
        ds = shifted((mine + whole * ds.astype(F32)).astype(BF16), "tensor", -1)

    dpi, dps, dd, small, tgi, tgs = call(
        functools.partial(back_kernel, heads),
        [((tokens, di), F32), ((tokens, sh), F32), ((tokens, 128), BF16), ((8, 128), F32), ((8, di), F32), ((8, sh), F32)],
        [((128, SPAN), F32), ((SPAN, 128), BF16), ((SPAN, 128), BF16), ((3, HALF, HALF), F32), ((SPAN, di), F32),
         ((SPAN, sh), F32)],
        xs, bc, draw, acs, bs, sin, fresh, dec, ds, vv, dy, rr, rawi, raws, ti, ts, dpar, skip, sel, selt, tri, triu,
        name="back",
    )

    hi = shifted(dpi.reshape(seqs, span, di)[:, :8], "tensor", -1)
    hs = shifted(dps.reshape(seqs, span, sh)[:, :8], "tensor", -1)
    ig, gi, gg, gsd, ng = call(
        last_kernel,
        [((tokens, dim), BF16), ((dim, di), BF16), ((dim, di), BF16), ((dim, sh + 128), BF16), ((8, dim), F32)],
        [((tokens, di), BF16), ((tokens, sh + 128), BF16)],
        x, c, gain, h, dpi, dps, hi, hs, dd, dgate, ti, ts, wi, wg, wsd, name="last",
    )

    parts = [g.reshape(dim, nt, dcol).transpose(1, 0, 2) for g in (gg, gi, go)]
    big = jnp.concatenate(parts, axis=2).reshape(nt * nd, rows, 3 * dcol)
    mine = lax.psum_scatter(big, both, scatter_dimension=0).astype(F32)
    gate_inner_grad = mine[:, : 2 * dcol].reshape(rows, 2, dcol)
    out_weight_grad = mine[:, 2 * dcol :].T
    gsd = lax.psum_scatter(gsd.reshape(nd, rows, sh + 128).astype(F32), "dp", scatter_dimension=0)
    gsd = lax.psum(gsd, "tensor")
    tgi, ggg, tgs, ng, small, skg = lax.psum((tgi, ggg, tgs, ng, small, skg), both)
    cut = lambda v: lax.dynamic_slice_in_dim(v, me * dcol, dcol, axis=-1)
    hcut = lambda v: lax.dynamic_slice_in_dim(v, me * hloc, hloc, axis=-1)
    return (
        out.reshape(block_input.shape),
        ig.reshape(block_input.shape),
        ng[0],
        gate_inner_grad,
        gsd[:, :sh],
        hcut(gsd[:, sh:]),
        cut(tgi[:4]),
        cut(tgi[4]),
        tgs[:4],
        tgs[4],
        hcut(small[0]),
        hcut(small[1]),
        hcut(skg[0]),
        cut(ggg[0]),
        out_weight_grad,
    )


def solution(mesh):
    placed = (
        P("dp", "tensor", None), P(), P("dp", None, "tensor"), P("dp", None), P("dp", "tensor"), P(None, "tensor"),
        P("tensor"), P(), P(), P("tensor"), P("tensor"), P("tensor"), P("tensor"), P("tensor", "dp"),
        P("dp", "tensor", None),
    )
    return jax.shard_map(
        local,
        mesh=mesh,
        in_specs=placed,
        out_specs=(
            P("dp", "tensor", None), P("dp", "tensor", None), P(), P("dp", None, "tensor"), P("dp", None),
            P("dp", "tensor"), P(None, "tensor"), P("tensor"), P(), P(), P("tensor"), P("tensor"), P("tensor"),
            P("tensor"), P("tensor", "dp"),
        ),
        check_vma=False,
    )
```

time: 1490 us -> 725 us (0.49)
  local copies, waits for them, and re-layouts: 369 us -> 65.1 us
  matrix products: 280 us -> 0 us
  other arithmetic: 285 us -> 20.4 us
  Pallas kernels: 0 us -> 129 us
  blocking collectives: 100 us -> 23.5 us
  waiting for transfers between devices: 414 us -> 436 us
  starting transfers between devices: 9 us -> 24.4 us
    dot_general x40 -> x0, matrix products: 267 us -> none  [the longest x8 103 us: scan_heads(): jnp.einsum('ctsh,cshp->cthp', scores, blocked_x, precision=TOP_PRECISION)]
    psum x1 -> x2, waiting for transfers between devices: 0.01 us -> 152 us  [the longest x1 122 us: local(): lax.psum((tgi, ggg, tgs, ng, small, skg), both)]
    reduce_scatter x3 -> x2, waiting for transfers between devices: 287 us -> 145 us  [the longest x1 122 us: local(): mine = lax.psum_scatter(big, both, scatter_dimension=0).astype(F32)]
    dynamic_slice x106 -> x5, local copies, waits for them, and re-layouts: 137 us -> 2.96 us  [the longest x3 1.76 us: local(): hcut = lambda v: lax.dynamic_slice_in_dim(v, me * hloc, hloc, axis=-1)]
    pallas_call x0 -> x4, Pallas kernels: none -> 129 us  [call(): pl.pallas_call(kernel, out_shape=[jax.ShapeDtypeStruct(s, d) for s, d in...]
    ppermute x0 -> x9, waiting for transfers between devices: none -> 93.2 us  [shifted(): lax.ppermute(v, axis, [(i, i + by) for i in range(n) if 0 <= i + by < n])]
    reduce_sum x35 -> x1, other arithmetic: 76.2 us -> 1.25 us  [local(): wd = jnp.sum(full[:, :, 3 * dcol:].astype(F32), axis=0).astype(BF16)]
    psum x4 -> x0, blocking collectives: 68.7 us -> none  [the longest x1 24.6 us: local(): lax.psum((conv_inner_grad, shift_inner_grad, decay_log_grad, delta_bias_g...]
  transfers between devices with their start and end apart: 9 -> 14, of which waited for: 4 -> 12; matrix products, arithmetic and copies ran while one was open for 18% -> 9% of each run, Pallas kernels for 0% -> 0%
where the time goes in v1:
time: 725 us; the launch traced here: 713 us
  waiting for transfers between devices  436 us (60%)
  Pallas kernels  129 us (18%)
  local copies, waits for them, and re-layouts  65.1 us (9%)
  starting transfers between devices  24.4 us (3%)
  blocking collectives  23.5 us (3%)
  other arithmetic  20.4 us (3%)
  between operations  14.4 us (2%)
    pallas_call x4, Pallas kernels, call(): pl.pallas_call(kernel, out_shape=[jax.ShapeDtypeStruct(s, d) for s, d in...  129 us
    psum x1, waiting for transfers between devices, local(): lax.psum((tgi, ggg, tgs, ng, small, skg), both)  122 us
    reduce_scatter x1, waiting for transfers between devices, local(): mine = lax.psum_scatter(big, both, scatter_dimension=0).astype(F32)  122 us
    ppermute x9, waiting for transfers between devices, shifted(): lax.ppermute(v, axis, [(i, i + by) for i in range(n) if 0 <= i + by < n])  93.2 us
    all_gather x1, waiting for transfers between devices, local(): full = lax.all_gather(pack, both, axis=0).reshape(nt, dim, 3 * dcol + 128)  44.9 us
    psum x1, waiting for transfers between devices, local(): gsd = lax.psum(gsd, 'tensor')  29.9 us
    ppermute x9, starting transfers between devices, shifted(): lax.ppermute(v, axis, [(i, i + by) for i in range(n) if 0 <= i + by < n])  24.2 us
    reduce_scatter x1, waiting for transfers between devices, local(): lax.psum_scatter(gsd.reshape(nd, rows, sh + 128).astype(F32), 'dp', scatt...  22.5 us
  transfers between devices with their start and end apart: 14, of which 12 were waited for; matrix products, arithmetic and copies ran while one was open for 9% of the time, Pallas kernels for 0%

profile of v1, /device:TPU:0, one launch (start us, length us, event | category | flops | bytes accessed | tf_op | source)
XLA Modules:
  0.0 712.8 jit_solution(11555413715896315706)
XLA Ops:
  12.1 5.1 collective-permute-start
  18.0 13.9 %all-gather.2 = f32[4,12,384]{2,1,0:T(8,128)S(1)} all-gather(f32[1,12,384]{2,1,0:T(8,128)S(1)} %maximum_bitcast_fusion), channel_id=3, replica_groups=mesh['dp'=8,'tensor'=4] {'tensor'}, dimensions={0}, use_global_device_ids=true | all-gather | bytes 92160 | tf_op jit(solution)/shard_map/all_gather | solution.py:505
  32.7 9.6 %all_gather.17 = bf16[768,256]{1,0:T(8,128)(2,1)S(1)} all-gather(bf16[96,256]{1,0:T(8,128)(2,1)S(1)} %copy-done.4), channel_id=1, replica_groups=mesh['dp'=8,'tensor'=4] {'dp'}, dimensions={0}, use_global_device_ids=true | all-gather | bytes 442368 | tf_op jit(solution)/shard_map/all_gather | solution.py:500
  45.2 44.9 %all-gather.5.cloned.1.call-done = bf16[3072,1280]{1,0:T(8,128)(2,1)} async-done(((bf16[96,1280]{1,0:T(8,128)(2,1)}), bf16[3072,1280]{1,0:T(8,128)(2,1)}) %all-gather.5.cloned.1.call-update) | async-done | bytes 7864336 | tf_op jit(solution)/shard_map/all_gather | solution.py:497
  91.3 5.3 fusion.25
  101.9 26.4 %front.1 = (bf16[1024,768]{1,0:T(8,128)(2,1)}, f32[2,528,1536]{2,1,0:T(8,128)}, f32[2,528,256]{2,1,0:T(8,128)}, bf16[1024,1536]{1,0:T(8,128)(2,1)}, bf16[1024,25...) custom-call(bf16[1024,768]{1,0:T(8,128)(2,1)} %bitcast.108, ...), custom_call_target="tpu_custom_call" | custom-call | tf_op jit(solution)/shard_map/front/pallas_call | solution.py:459
  129.2 2.2 add_convert_fusion.5
  131.5 3.5 collective-permute-start.1
  134.9 17.2 %collective-permute-done.1 = bf16[2,128,1536]{2,1,0:T(8,128)(2,1)S(1)} collective-permute-done((bf16[2,128,1536]{2,1,0:T(8,128)(2,1)S(1)}, bf16[2,128,1536]{2,1,0:T(8,128)(2,1)S(1)}, u32[]{:S(2)}, u32[]{:S(2)}) %collective-permute-start.1) | collective-permute-done | bytes 786464 | tf_op jit(solution)/shard_map/ppermute | solution.py:472
  152.3 4.4 collective-permute-start.2
  156.8 16.3 %collective-permute-done.2 = bf16[2,128,1536]{2,1,0:T(8,128)(2,1)S(1)} collective-permute-done((bf16[2,128,1536]{2,1,0:T(8,128)(2,1)S(1)}, bf16[2,128,1536]{2,1,0:T(8,128)(2,1)S(1)}, u32[]{:S(2)}, u32[]{:S(2)}) %collective-permute-start.2) | collective-permute-done | bytes 786464 | tf_op jit(solution)/shard_map/ppermute | solution.py:472
  174.2 4.6 collective-permute-start.3
  181.4 3.5 copy.75
  190.2 4.2 collective-permute-done.3.sin_ref
  195.3 36.0 %mid.1 = (bf16[1024,768]{1,0:T(8,128)(2,1)}, bf16[1024,1536]{1,0:T(8,128)(2,1)}, bf16[1024,1536]{1,0:T(8,128)(2,1)}, bf16[1024,1536]{1,0:T(8,128)(2,1)}, f32[102...) custom-call(bf16[1024,768]{1,0:T(8,128)(2,1)} %bitcast.109, ...), custom_call_target="tpu_custom_call" | custom-call | tf_op jit(solution)/shard_map/mid/pallas_call | solution.py:459
  231.4 2.2 add_convert_fusion.2
  234.9 18.3 %collective-permute-done.4 = bf16[2,128,1536]{2,1,0:T(8,128)(2,1)S(1)} collective-permute-done((bf16[2,128,1536]{2,1,0:T(8,128)(2,1)S(1)}, bf16[2,128,1536]{2,1,0:T(8,128)(2,1)S(1)}, u32[]{:S(2)}, u32[]{:S(2)}) %collective-permute-start.4) | collective-permute-done | bytes 786464 | tf_op jit(solution)/shard_map/ppermute | solution.py:472
  254.7 17.0 %collective-permute-done.5 = bf16[2,128,1536]{2,1,0:T(8,128)(2,1)S(1)} collective-permute-done((bf16[2,128,1536]{2,1,0:T(8,128)(2,1)S(1)}, bf16[2,128,1536]{2,1,0:T(8,128)(2,1)S(1)}, u32[]{:S(2)}, u32[]{:S(2)}) %collective-permute-start.5) | collective-permute-done | bytes 786464 | tf_op jit(solution)/shard_map/ppermute | solution.py:472
  273.9 15.4 %collective-permute-done.6.ds_ref = bf16[2,128,1536]{2,1,0:T(8,128)(2,1)S(1)} collective-permute-done((bf16[2,128,1536]{2,1,0:T(8,128)(2,1)S(1)}, bf16[2,128,1536]{2,1,0:T(8,128)(2,1)S(1)}, u32[]{:S(2)}, u32[]{:S(2)}) %collective-permute-start.6) | collective-permute-done | bytes 786464 | tf_op jit(solution)/shard_map/ppermute | solution.py:472
  290.2 44.1 %back.1 = (f32[1024,1536]{1,0:T(8,128)}, f32[1024,256]{1,0:T(8,128)}, bf16[1024,128]{1,0:T(8,128)(2,1)}, f32[8,128]{1,0:T(8,128)}, f32[8,1536]{1,0:T(8,128)}, /*index=5*/f32[8,256]{1,0:T(8,128)}) custom-call(bf16[1024,1536]{1,0:T(8,128)(2,1)} %get-tuple-element.45.xs_ref, bf16[1024,256]{1,0:T(8,128)(2,1)} %get-tuple-element.46.bc_ref, ...), custom_call_target="tpu_custom_call" | custom-call | tf_op jit(solution)/shard_map/back/pallas_call | solution.py:459
  338.7 4.8 collective-permute-done.8.hs_ref
  344.2 22.6 %last.1 = (bf16[1024,768]{1,0:T(8,128)(2,1)}, bf16[768,1536]{1,0:T(8,128)(2,1)}, bf16[768,1536]{1,0:T(8,128)(2,1)}, bf16[768,384]{1,0:T(8,128)(2,1)}, f32[8,768]{1,0:T(8,128)}) custom-call(bf16[1024,768]{1,0:T(8,128)(2,1)} %bitcast.110, bf16[1024,768]{1,0:T(8,128)(2,1)} %bitcast.123, f32[1,768]{1,0:T(1,128)} %broadcast_in_dim.29.gain_ref, ...), custom_call_target="tpu_custom_call" | custom-call | tf_op jit(solution)/shard_map/last/pallas_call | solution.py:459
  366.8 2.6 copy.69
  370.2 4.2 reshape.204
  374.3 5.2 reshape.202
  379.6 5.2 reshape.203
  384.8 22.5 %reduce-scatter.5.cloned.1.call-done = f32[1,96,384]{1,2,0:T(8,128)} async-done(((f32[8,96,384]{1,2,0:T(8,128)}), f32[1,96,384]{1,2,0:T(8,128)}) %reduce-scatter.5.cloned.1.call-update) | async-done | bytes 147472 | tf_op jit(solution)/shard_map/reduce_scatter | solution.py:586
  407.4 4.8 pad_maximum_fusion
  412.2 3.8 copy.68
  416.0 122.3 %all-reduce.10.cloned.1.call-done = (f32[8,768]{1,0:T(8,128)}, f32[8,1536]{1,0:T(8,128)}, f32[8,256]{1,0:T(8,128)}, f32[8,128]{1,0:T(8,128)}, f32[8,128]{1,0:T(8,128)}, /*index=5*/f32[8,1536]{1,0:T(8,128)}) async-done(((f32[8,768]{1,0:T(8,128)}, f32[8,1536]{1,0:T(8,128)}, f32[8,256]{1,0:T(8,128)}, f32[8,128]{1,0:T(8,128)}, f32[8,128]{1,0:T(8,128)}, /*index=5*/f32[8,1536]{1,0:T(8,128)}), ...) | async-done | bytes 139280 | tf_op jit(solution)/shard_map/psum | solution.py:588
  548.4 29.9 %all-reduce.8.cloned.1.call-done = f32[96,384]{0,1:T(8,128)} async-done(((f32[96,384]{0,1:T(8,128)}), f32[96,384]{0,1:T(8,128)}) %all-reduce.8.cloned.1.call-update) | async-done | bytes 147472 | tf_op jit(solution)/shard_map/psum | solution.py:587
  581.4 122.2 %reduce-scatter.3.cloned.1.call-done = bf16[1,96,1152]{2,1,0:T(8,128)(2,1)} async-done(((bf16[32,96,1152]{2,1,0:T(8,128)(2,1)}), bf16[1,96,1152]{2,1,0:T(8,128)(2,1)}) %reduce-scatter.3.cloned.1.call-update) | async-done | bytes 221200 | tf_op jit(solution)/shard_map/reduce_scatter | solution.py:583
  (119 shorter events, 54.2 us)
Async XLA Ops:
  7.2 10.1 %copy-start.14 = (bf16[256]{0:T(256)(128)(2,1)S(1)}, bf16[256]{0:T(256)(128)(2,1)}, u32[]{:S(2)}) copy-start(bf16[256]{0:T(256)(128)(2,1)} %param.23) | copy-start | bytes 1540
  7.2 10.1 %copy-start.10 = (bf16[384]{0:T(512)(128)(2,1)S(1)}, bf16[384]{0:T(512)(128)(2,1)}, u32[]{:S(2)}) copy-start(bf16[384]{0:T(512)(128)(2,1)} %param.21) | copy-start | bytes 2308
  7.2 10.1 %copy-start.8 = (f32[384]{0:T(512)S(1)}, f32[384]{0:T(512)}, u32[]{:S(2)}) copy-start(f32[384]{0:T(512)} %param.27) | copy-start | bytes 4612
  7.2 10.1 %copy-start.6 = (f32[768]{0:T(1024)S(1)}, f32[768]{0:T(1024)}, u32[]{:S(2)}) copy-start(f32[768]{0:T(1024)} %param.16) | copy-start | bytes 9220
  7.2 10.7 %copy-start.7 = (bf16[4,384]{1,0:T(4,128)(2,1)S(1)}, bf16[4,384]{1,0:T(4,128)(2,1)}, u32[]{:S(2)}) copy-start(bf16[4,384]{1,0:T(4,128)(2,1)} %param.20) | copy-start | bytes 9220
  7.2 10.7 %copy-start.11 = (f32[6]{0:T(128)S(1)}, f32[6]{0:T(128)}, u32[]{:S(2)}) copy-start(f32[6]{0:T(128)} %param.26) | copy-start | bytes 76
  7.2 10.7 %copy-start.12 = (f32[6]{0:T(128)S(1)}, f32[6]{0:T(128)}, u32[]{:S(2)}) copy-start(f32[6]{0:T(128)} %param.25) | copy-start | bytes 76
  7.3 10.7 %copy-start.13 = (f32[6]{0:T(128)S(1)}, f32[6]{0:T(128)}, u32[]{:S(2)}) copy-start(f32[6]{0:T(128)} %param.24) | copy-start | bytes 76
  7.3 25.5 %copy-start.4 = (bf16[96,256]{1,0:T(8,128)(2,1)S(1)}, bf16[96,256]{1,0:T(8,128)(2,1)}, u32[]{:S(2)}) copy-start(bf16[96,256]{1,0:T(8,128)(2,1)} %param.18) | copy-start | bytes 147460
  7.3 35.6 %copy-start.9 = (bf16[4,256]{1,0:T(4,128)(2,1)S(1)}, bf16[4,256]{1,0:T(4,128)(2,1)}, u32[]{:S(2)}) copy-start(bf16[4,256]{1,0:T(4,128)(2,1)} %param.22) | copy-start | bytes 6148
  7.3 82.8 %all-gather.5.cloned.1.call-start = ((), (), s32[]{:S(2)}) async-start(), calls=%async_computation.5 | async-start | bytes 8110080 | tf_op jit(solution)/shard_map/all_gather | solution.py:497
  11.3 396.1 %reduce-scatter.5.cloned.1.call-start = ((), (), s32[]{:S(2)}) async-start(), calls=%async_computation.3 | async-start | bytes 1769472 | tf_op jit(solution)/shard_map/reduce_scatter | solution.py:586
  12.1 89.1 %collective-permute-start = (bf16[2,16,768]{2,1,0:T(8,128)(2,1)S(1)}, bf16[2,16,768]{2,1,0:T(8,128)(2,1)S(1)}, u32[]{:S(2)}, u32[]{:S(2)}) collective-permute-start(bf16[2,16,768]{2,1,0:T(8,128)(2,1)S(1)} %slice.121), channel_id=1, source_target_pairs={{0,1},{1,2},{2,3},{4,5},{5,6},{6,7},{8,9},{9,10},{10,11},{12,13},{... | collective-permute-start | bytes 147464 | tf_op jit(solution)/shard_map/ppermute | solution.py:472
  101.2 0.6 copy-start.3
  131.5 20.6 %collective-permute-start.1 = (bf16[2,128,1536]{2,1,0:T(8,128)(2,1)S(1)}, bf16[2,128,1536]{2,1,0:T(8,128)(2,1)S(1)}, u32[]{:S(2)}, u32[]{:S(2)}) collective-permute-start(bf16[2,128,1536]{2,1,0:T(8,128)(2,1)S(1)} %get-tuple-element.129), channel_id=1, source_target_pairs={{0,1},{1,2},{2,3},{4,5},{5,6},{6,7},{8,9},{9,10},{10,11},{12,13},{... | collective-permute-start | bytes 2359304 | tf_op jit(solution)/shard_map/ppermute | solution.py:472
  152.3 20.8 %collective-permute-start.2 = (bf16[2,128,1536]{2,1,0:T(8,128)(2,1)S(1)}, bf16[2,128,1536]{2,1,0:T(8,128)(2,1)S(1)}, u32[]{:S(2)}, u32[]{:S(2)}) collective-permute-start(bf16[2,128,1536]{2,1,0:T(8,128)(2,1)S(1)} %add_convert_fusion.4), channel_id=1, source_target_pairs={{0,1},{1,2},{2,3},{4,5},{5,6},{6,7},{8,9},{9,10},{10,11},{12,13},{... | collective-permute-start | bytes 2359304 | tf_op jit(solution)/shard_map/ppermute | solution.py:472
  174.2 20.2 %collective-permute-start.3 = (bf16[2,128,1536]{2,1,0:T(8,128)(2,1)}, bf16[2,128,1536]{2,1,0:T(8,128)(2,1)S(1)}, u32[]{:S(2)}, u32[]{:S(2)}) collective-permute-start(bf16[2,128,1536]{2,1,0:T(8,128)(2,1)} %add_convert_fusion.3), channel_id=1, source_target_pairs={{0,1},{1,2},{2,3},{4,5},{5,6},{6,7},{8,9},{9,10},{10,11},{12,13},{... | collective-permute-start | bytes 2359304 | tf_op jit(solution)/shard_map/ppermute | solution.py:472
  194.4 0.9 copy-start
  233.6 19.6 %collective-permute-start.4 = (bf16[2,128,1536]{2,1,0:T(8,128)(2,1)S(1)}, bf16[2,128,1536]{2,1,0:T(8,128)(2,1)S(1)}, u32[]{:S(2)}, u32[]{:S(2)}) collective-permute-start(bf16[2,128,1536]{2,1,0:T(8,128)(2,1)S(1)} %get-tuple-element.127), channel_id=1, source_target_pairs={{1,0},{2,1},{3,2},{5,4},{6,5},{7,6},{9,8},{10,9},{11,10},{13,12},{... | collective-permute-start | bytes 2359304 | tf_op jit(solution)/shard_map/ppermute | solution.py:472
  253.4 18.3 %collective-permute-start.5 = (bf16[2,128,1536]{2,1,0:T(8,128)(2,1)S(1)}, bf16[2,128,1536]{2,1,0:T(8,128)(2,1)S(1)}, u32[]{:S(2)}, u32[]{:S(2)}) collective-permute-start(bf16[2,128,1536]{2,1,0:T(8,128)(2,1)S(1)} %add_convert_fusion.1), channel_id=1, source_target_pairs={{1,0},{2,1},{3,2},{5,4},{6,5},{7,6},{9,8},{10,9},{11,10},{13,12},{... | collective-permute-start | bytes 2359304 | tf_op jit(solution)/shard_map/ppermute | solution.py:472
  272.0 17.4 %collective-permute-start.6 = (bf16[2,128,1536]{2,1,0:T(8,128)(2,1)S(1)}, bf16[2,128,1536]{2,1,0:T(8,128)(2,1)S(1)}, u32[]{:S(2)}, u32[]{:S(2)}) collective-permute-start(bf16[2,128,1536]{2,1,0:T(8,128)(2,1)S(1)} %add_convert_fusion), channel_id=1, source_target_pairs={{1,0},{2,1},{3,2},{5,4},{6,5},{7,6},{9,8},{10,9},{11,10},{13,12},{... | collective-permute-start | bytes 2359304 | tf_op jit(solution)/shard_map/ppermute | solution.py:472
  289.3 0.9 copy-start.1
  335.3 8.3 %collective-permute-start.7 = (f32[2,8,1536]{2,1,0:T(8,128)S(1)}, f32[2,8,1536]{2,1,0:T(8,128)S(1)}, u32[]{:S(2)}, u32[]{:S(2)}) collective-permute-start(f32[2,8,1536]{2,1,0:T(8,128)S(1)} %slice.176), channel_id=1, source_target_pairs={{1,0},{2,1},{3,2},{5,4},{6,5},{7,6},{9,8},{10,9},{11,10},{13,12},{... | collective-permute-start | bytes 294920 | tf_op jit(solution)/shard_map/ppermute | solution.py:472
  337.3 6.2 collective-permute-start.8
  343.5 0.6 copy-start.5
  343.5 0.6 copy-start.2
  369.4 168.9 %all-reduce.10.cloned.1.call-start = ((), (), s32[]{:S(2)}) async-start(), calls=%async_computation.6 | async-start | bytes 278528 | tf_op jit(solution)/shard_map/psum | solution.py:588
  370.1 208.2 %all-reduce.8.cloned.1.call-start = ((), (), s32[]{:S(2)}) async-start(), calls=%async_computation.4 | async-start | bytes 393216 | tf_op jit(solution)/shard_map/psum | solution.py:587
  407.4 296.2 %reduce-scatter.3.cloned.1.call-start = ((), (), s32[]{:S(2)}) async-start(), calls=%async_computation.2 | async-start | bytes 7299072 | tf_op jit(solution)/shard_map/reduce_scatter | solution.py:583
Sparse Core Ops, SparseCore 0:
  11.6 78.4 all-gather.4
  369.5 37.8 reduce-scatter.4
  414.9 123.3 all-reduce.9
  540.5 37.7 all-reduce.7
  584.8 118.7 reduce-scatter.2

commit v2 on v1

--- a/solution.py
+++ b/solution.py
@@ -77,8 +77,8 @@
 
 
 def front_kernel(
-    heads,
-    x_ref, xh_ref, gain_ref, wi_ref, wsd_ref, ti_ref, ts_ref, dpar_ref, sel_ref, tri_ref,
+    heads, nt,
+    x_ref, xh_ref, gain_ref, w1_ref, ws_ref, ti_ref, ts_ref, dpar_ref, sel_ref, tri_ref,
     h_ref, rawi_ref, raws_ref, xs_ref, bc_ref, draw_ref, acs_ref, bs_ref, fresh_ref, dec_ref,
     hh_ref, w_ref,
 ):
@@ -93,9 +93,13 @@
         return (v * lax.rsqrt(jnp.mean(v * v, axis=-1, keepdims=True) + EPSILON) * gain_ref[...]).astype(BF16)
 
     hh_ref[...] = norm(xh_ref[...])
+    part = w1_ref.shape[1] // nt
     for s in range(seqs):
-        rawi_ref[s, 0:16, :] = dot(hh_ref[16 * s : 16 * s + 16, :], wi_ref[...])
-        raws_ref[s, 0:16, :] = dot(hh_ref[16 * s : 16 * s + 16, :], wsd_ref[:, :sh])
+        rows = slice(16 * s, 16 * s + 16)
+        for t in range(nt):
+            own = dot(hh_ref[rows, :], w1_ref[:, part * t : part * (t + 1) - 128])
+            rawi_ref[s, 0:16, (part - 128) * t : (part - 128) * (t + 1)] = own
+        raws_ref[s, 0:16, :] = dot(hh_ref[rows, :], ws_ref[...])
 
     def seq_step(s, carry):
         def norm_step(b, c):
@@ -105,11 +109,14 @@
 
         lax.fori_loop(0, per, norm_step, 0)
         rows = block_rows(s, span)
-        for c0 in range(0, di, WIDE):
-            rawi_ref[s, 16:ext, c0 : c0 + WIDE] = dot(h_ref[rows, :], wi_ref[:, c0 : c0 + WIDE])
-        sd = dot(h_ref[rows, :], wsd_ref[...])
-        raws_ref[s, 16:ext, :] = sd[:, :sh]
-        draw_ref[rows, :] = sd[:, sh:] + dpar_ref[0:1, :]
+        part = w1_ref.shape[1] // nt
+        draw = dpar_ref[0:1, :]
+        for t in range(nt):
+            both = dot(h_ref[rows, :], w1_ref[:, part * t : part * (t + 1)])
+            rawi_ref[s, 16:ext, (part - 128) * t : (part - 128) * (t + 1)] = both[:, : part - 128]
+            draw = draw + both[:, part - 128 :]
+        draw_ref[rows, :] = draw
+        raws_ref[s, 16:ext, :] = dot(h_ref[rows, :], ws_ref[...])
 
         def conv(raw, par, out, cols):
             def step(r, c):
@@ -401,19 +408,24 @@
 
 
 def last_kernel(
+    nt,
     x_ref, c_ref, gain_ref, h_ref, dpi_ref, dps_ref, hi_ref, hs_ref, dd_ref, dgate_ref, ti_ref, ts_ref,
-    wi_ref, wg_ref, wsd_ref,
-    ig_ref, gi_ref, gg_ref, gsd_ref, ng_ref,
-    din_ref, dsd_ref,
+    w1_ref, w2_ref, ws_ref,
+    ig_ref, g1_ref, g2_ref, ng_ref,
+    din_ref,
 ):
     tokens, di = dgate_ref.shape
     seqs = hi_ref.shape[0]
     span = tokens // seqs
     sh = dps_ref.shape[1]
+    part = w1_ref.shape[1] // nt
+    inner = part * nt
     ng_ref[...] = jnp.zeros_like(ng_ref)
-    dsd_ref[:, sh:] = dd_ref[...]
-
-    def conv_t(dpre, halo, par, out, cols):
+    for t in range(nt):
+        din_ref[:, part * (t + 1) - 128 : part * (t + 1)] = dd_ref[...]
+
+    def conv_t(dpre, halo, par, c0, to):
+        cols = slice(c0, c0 + 128)
         for s in range(seqs):
             for r0 in range(0, span, HALF):
                 base = s * span + r0
@@ -426,24 +438,25 @@
                 acc = par[3:4, cols] * v[0:HALF]
                 for k in range(3):
                     acc = acc + par[k : k + 1, cols] * v[3 - k : 3 - k + HALF]
-                out[base : base + HALF, cols] = acc.astype(BF16)
-
-    for c0 in range(0, di, 256):
-        conv_t(dpi_ref, hi_ref, ti_ref, din_ref, slice(c0, c0 + 256))
-    for c0 in range(0, sh, 256):
-        conv_t(dps_ref, hs_ref, ts_ref, dsd_ref, slice(c0, c0 + 256))
-
+                din_ref[base : base + HALF, to : to + 128] = acc.astype(BF16)
+
+    for c0 in range(0, di, 128):
+        t = c0 // (part - 128)
+        conv_t(dpi_ref, hi_ref, ti_ref, c0, part * t + c0 - (part - 128) * t)
+    for c0 in range(0, sh, 128):
+        conv_t(dps_ref, hs_ref, ts_ref, c0, inner + c0)
+
+    for c0 in range(0, inner, WIDE):
+        g1_ref[:, c0 : c0 + WIDE] = dot_tn(h_ref[...], din_ref[:, c0 : c0 + WIDE]).astype(BF16)
+    g1_ref[:, inner:] = dot_tn(h_ref[...], din_ref[:, inner:]).astype(BF16)
     for c0 in range(0, di, WIDE):
-        cols = slice(c0, c0 + WIDE)
-        gi_ref[:, cols] = dot_tn(h_ref[...], din_ref[:, cols]).astype(BF16)
-        gg_ref[:, cols] = dot_tn(h_ref[...], dgate_ref[:, cols]).astype(BF16)
-    gsd_ref[...] = dot_tn(h_ref[...], dsd_ref[...]).astype(BF16)
+        g2_ref[:, c0 : c0 + WIDE] = dot_tn(h_ref[...], dgate_ref[:, c0 : c0 + WIDE]).astype(BF16)
 
     def step(b, carry):
         rows = block_rows(b, SPAN)
-        dh = dot_nt(dgate_ref[rows, :], wg_ref[...])
-        dh = dh + dot_nt(din_ref[rows, :], wi_ref[...])
-        dh = dh + dot_nt(dsd_ref[rows, :], wsd_ref[...])
+        dh = dot_nt(dgate_ref[rows, :], w2_ref[...])
+        dh = dh + dot_nt(din_ref[rows, :inner], w1_ref[...])
+        dh = dh + dot_nt(din_ref[rows, inner:], ws_ref[...])
         u = x_ref[rows, :].astype(F32)
         r1 = lax.rsqrt(jnp.mean(u * u, axis=-1, keepdims=True) + EPSILON)
         ng_ref[0:1, :] += jnp.sum(dh * u * r1, axis=0, keepdims=True)
@@ -455,21 +468,447 @@
     lax.fori_loop(0, tokens // SPAN, step, 0)
 
 
-def call(kernel, outs, scratch, *args, name):
+MESH = pl.DeviceIdType.MESH
+
+
+class Sends:
+    def __init__(self, send, recv):
+        self.send, self.recv, self.used, self.started = send, recv, 0, []
+
+    def make(self, src, dst, to):
+        k = self.used
+        self.used += 1
+        return pltpu.make_async_remote_copy(
+            src_ref=src, dst_ref=dst, send_sem=self.send.at[k], recv_sem=self.recv.at[k],
+            device_id=to, device_id_type=MESH,
+        )
+
+    def start(self, src, dst, to):
+        copy = self.make(src, dst, to)
+        copy.start()
+        self.started.append(copy)
+        return copy
+
+    def finish(self):
+        for copy in self.started:
+            copy.wait_send()
+
+
+def greet(others):
+    barrier = pltpu.get_barrier_semaphore()
+    for to in others:
+        pl.semaphore_signal(barrier, inc=1, device_id=to, device_id_type=MESH)
+    pl.semaphore_wait(barrier, len(others))
+
+
+def place():
+    z = lax.axis_index("tensor")
+    d = lax.axis_index("dp")
+    core = lax.rem(d, 2)
+    x = lax.rem(d // 2, 2)
+    y = d // 4
+    return z, d, core, x, y
+
+
+def xor_peer(core, x, y, k):
+    c1 = 1 - core if k & 1 else core
+    x1 = 1 - x if k & 2 else x
+    y1 = 1 - y if k & 4 else y
+    return y1 * 4 + x1 * 2 + c1
+
+
+def dp_rows(d, size, part=None):
+    if part is None:
+        return pl.ds(pl.multiple_of(d * size, 16), size)
+    return pl.ds(pl.multiple_of(d * size + part * (size // 2), 16), size // 2)
+
+
+def columns(t, size):
+    return pl.ds(pl.multiple_of(t * size, 128), size)
+
+
+class Gather:
+    MESSAGES = 13
+
+    def __init__(self, sends, nt, shard, full, here):
+        self.sends, self.nt, self.shard, self.full = sends, nt, shard, full
+        self.z, self.d, self.core, self.x, self.y = here
+        self.rows, self.width = shard.shape
+
+    def to(self, k):
+        return {"dp": xor_peer(self.core, self.x, self.y, k)}
+
+    def ref(self, k, part=None):
+        return self.full.at[dp_rows(xor_peer(self.core, self.x, self.y, k), self.rows, part), :]
+
+    def begin(self, sem):
+        mine = self.full.at[dp_rows(self.d, self.rows), columns(self.z, self.width)]
+        self.local = pltpu.make_async_copy(self.shard, mine, sem)
+        self.local.start()
+        self.zs = []
+        for dz in range(1, self.nt):
+            to = {"tensor": lax.rem(self.z + dz, self.nt)}
+            self.zs.append(self.sends.start(self.shard, mine, to))
+
+    def column(self):
+        self.local.wait()
+        for copy in self.zs:
+            copy.wait_recv()
+        own_a, own_b = self.ref(0, 0), self.ref(0, 1)
+        self.x0 = self.sends.start(own_a, own_a, self.to(2))
+        self.y0 = self.sends.start(own_b, own_b, self.to(4))
+        self.c = [self.sends.start(self.ref(0), self.ref(0), self.to(1))]
+        self.y1 = self.sends.start(own_a, own_a, self.to(4))
+        self.x1 = self.sends.start(own_b, own_b, self.to(2))
+
+    def forward(self):
+        self.x0.wait_recv()
+        self.y2 = self.sends.start(self.ref(2, 0), self.ref(2, 0), self.to(4))
+        self.y0.wait_recv()
+        self.x2 = self.sends.start(self.ref(4, 1), self.ref(4, 1), self.to(2))
+        self.x1.wait_recv()
+        self.c.append(self.sends.start(self.ref(2), self.ref(2), self.to(1)))
+        self.y1.wait_recv()
+        self.c.append(self.sends.start(self.ref(4), self.ref(4), self.to(1)))
+
+    def corner(self):
+        self.y2.wait_recv()
+        self.x2.wait_recv()
+        self.c.append(self.sends.start(self.ref(6), self.ref(6), self.to(1)))
+
+    def finish(self):
+        for copy in self.c:
+            copy.wait_recv()
+
+
+def gather_kernel(
+    nt, w1_ref, w2_ref, w3_ref, ws_ref, par_ref, xl_ref,
+    f1_ref, f2_ref, f3_ref, fs_ref, fp_ref, xh_ref,
+    send, recv, local,
+):
+    here = place()
+    z, d, core, x, y = here
+    sends = Sends(send, recv)
+    others = [{"tensor": lax.rem(z + dz, nt)} for dz in range(1, nt)]
+    others += [{"dp": xor_peer(core, x, y, k)} for k in range(1, 8)]
+    greet(others)
+    rows = ws_ref.shape[0]
+    secs = [Gather(sends, nt, a, b, here) for a, b in ((w1_ref, f1_ref), (w2_ref, f2_ref), (w3_ref, f3_ref))]
+    secs[0].begin(local.at[0])
+    mine = fs_ref.at[dp_rows(d, rows), :]
+    own = [pltpu.make_async_copy(ws_ref, mine, local.at[3]), pltpu.make_async_copy(par_ref, fp_ref.at[z], local.at[4])]
+    for copy in own:
+        copy.start()
+    got = [sends.start(ws_ref, mine, {"dp": xor_peer(core, x, y, k)}) for k in range(1, 8)]
+    got += [sends.start(par_ref, fp_ref.at[z], {"tensor": lax.rem(z + dz, nt)}) for dz in range(1, nt)]
+    edge = sends.make(xl_ref, xh_ref, {"tensor": lax.rem(z + 1, nt)})
+
+    @pl.when(z < nt - 1)
+    def _():
+        edge.start()
+
+    for k in (1, 2):
+        secs[k].begin(local.at[k])
+    for sec in secs:
+        sec.column()
+        sec.forward()
+    for sec in secs:
+        sec.corner()
+    for copy in own:
+        copy.wait()
+    for copy in got:
+        copy.wait_recv()
+
+    @pl.when(z > 0)
+    def _():
+        edge.wait_recv()
+
+    @pl.when(z == 0)
+    def _():
+        xh_ref[...] = jnp.zeros_like(xh_ref)
+
+    for sec in secs:
+        sec.finish()
+    sends.finish()
+
+    @pl.when(z < nt - 1)
+    def _():
+        edge.wait_send()
+
+
+def chain_kernel(nt, by, mine_ref, whole_ref, got_ref, out_ref, send, recv):
+    z = lax.axis_index("tensor")
+    seqs, _, di = got_ref.shape
+    has_prev = z > 0 if by > 0 else z < nt - 1
+    has_next = z < nt - 1 if by > 0 else z > 0
+    prev = {"tensor": lax.rem(z - by + nt, nt)}
+    nxt = {"tensor": lax.rem(z + by + nt, nt)}
+    greet((prev, nxt))
+
+    @pl.when(jnp.logical_not(has_prev))
+    def _():
+        got_ref[...] = jnp.zeros_like(got_ref)
+
+    sends = Sends(send, recv)
+    copies = []
+    for s in range(seqs):
+        for c0 in range(0, di, WIDE):
+            cols = slice(c0, c0 + WIDE)
+            copy = sends.make(out_ref.at[s, :, cols], got_ref.at[s, :, cols], nxt)
+            copies.append(copy)
+
+            @pl.when(has_prev)
+            def _(copy=copy):
+                copy.wait_recv()
+
+            @pl.when(has_next)
+            def _(copy=copy, s=s, cols=cols):
+                out_ref[s, :, cols] = (
+                    mine_ref[s, :, cols] + whole_ref[s, 0:1, cols] * got_ref[s, :, cols].astype(F32)
+                ).astype(BF16)
+                copy.start()
+
+    for copy in copies:
+
+        @pl.when(has_next)
+        def _(copy=copy):
+            copy.wait_send()
+
+
+class Reduce:
+    MESSAGES = 24
+
+    @staticmethod
+    def scratch(rows, width, nt, wz):
+        half = rows // 2
+        shapes = [(4, rows, width)] * 2 + [(2, half, width)] * 4 + [(half, width)] * 2 + [(rows, width), (nt, rows, wz)]
+        return [pltpu.VMEM(s, BF16) for s in shapes]
+
+    def __init__(self, sends, nt, g, bufs, cuts, here):
+        self.sends, self.nt, self.g, self.cuts = sends, nt, g, cuts
+        self.rc, self.p, self.ra, self.rb, self.qa, self.qb, self.ta, self.tb, self.f, self.rz = bufs
+        self.z, self.d, self.core, self.x, self.y = here
+        self.rows = self.p.shape[1]
+        self.half = self.rows // 2
+
+    def to(self, k):
+        return {"dp": xor_peer(self.core, self.x, self.y, k)}
+
+    def begin(self):
+        self.got = []
+        for q in range(4):
+            src = self.g.at[dp_rows(2 * q + 1 - self.core, self.rows), :]
+            self.got.append(self.sends.start(src, self.rc.at[q], self.to(1)))
+
+    def first(self):
+        h = self.half
+        for q in range(4):
+            self.got[q].wait_recv()
+            own = self.g[dp_rows(2 * q + self.core, self.rows), :].astype(F32)
+            self.p[q] = (own + self.rc[q].astype(F32)).astype(BF16)
+        self.a = []
+        self.b = []
+        for i in range(2):
+            src = self.p.at[2 * i + 1 - self.x, pl.ds(0, h), :]
+            self.a.append(self.sends.start(src, self.ra.at[i], self.to(2)))
+            src = self.p.at[2 * (1 - self.y) + i, pl.ds(h, h), :]
+            self.b.append(self.sends.start(src, self.rb.at[i], self.to(4)))
+
+    def second(self):
+        h = self.half
+        for i in range(2):
+            self.a[i].wait_recv()
+            own = self.p[2 * i + self.x, 0:h, :].astype(F32)
+            self.qa[i] = (own + self.ra[i].astype(F32)).astype(BF16)
+            self.b[i].wait_recv()
+            own = self.p[2 * self.y + i, h:, :].astype(F32)
+            self.qb[i] = (own + self.rb[i].astype(F32)).astype(BF16)
+        self.a2 = self.sends.start(self.qa.at[1 - self.y], self.ta, self.to(4))
+        self.b2 = self.sends.start(self.qb.at[1 - self.x], self.tb, self.to(2))
+
+    def third(self):
+        h = self.half
+        self.a2.wait_recv()
+        self.f[0:h, :] = (self.qa[self.y].astype(F32) + self.ta[...].astype(F32)).astype(BF16)
+        self.b2.wait_recv()
+        self.f[h:, :] = (self.qb[self.x].astype(F32) + self.tb[...].astype(F32)).astype(BF16)
+        self.zs = []
+        at = 0
+        for first, size, by_t in self.cuts:
+            dst = self.rz.at[self.z, :, pl.ds(at, size)]
+            for dz in range(1, self.nt):
+                t = lax.rem(self.z + dz, self.nt)
+                src = self.f.at[:, columns(t, size) if by_t else pl.ds(first, size)]
+                self.zs.append(self.sends.start(src, dst, {"tensor": t}))
+            self.rz[self.z, :, at : at + size] = self.f[:, columns(self.z, size) if by_t else pl.ds(first, size)]
+            at += size
+
+    def last(self):
+        for copy in self.zs:
+            copy.wait_recv()
+        total = self.rz[0].astype(F32)
+        for t in range(1, self.nt):
+            total = total + self.rz[t].astype(F32)
+        return total
+
+
+class SmallSum:
+    MESSAGES = 6
+
+    @staticmethod
+    def scratch(shape, nt):
+        return [pltpu.VMEM((3,) + shape, F32), pltpu.VMEM((3,) + shape, F32), pltpu.VMEM((nt,) + shape, F32)]
+
+    def __init__(self, sends, nt, v, bufs, here):
+        self.sends, self.nt, self.v = sends, nt, v
+        self.own, self.got, self.rz = bufs
+        self.z, self.d, self.core, self.x, self.y = here
+
+    def begin(self):
+        self.own[0] = self.v[...]
+        self.copy = self.sends.start(self.own.at[0], self.got.at[0], {"dp": xor_peer(self.core, self.x, self.y, 1)})
+
+    def step(self, k):
+        self.copy.wait_recv()
+        total = self.own[k - 1] + self.got[k - 1]
+        if k < 3:
+            self.own[k] = total
+            self.copy = self.sends.start(
+                self.own.at[k], self.got.at[k], {"dp": xor_peer(self.core, self.x, self.y, 2**k)}
+            )
+        else:
+            self.rz[self.z] = total
+            self.zs = [
+                self.sends.start(self.rz.at[self.z], self.rz.at[self.z], {"tensor": lax.rem(self.z + dz, self.nt)})
+                for dz in range(1, self.nt)
+            ]
+
+    def last(self):
+        for copy in self.zs:
+            copy.wait_recv()
+        total = self.rz[0]
+        for t in range(1, self.nt):
+            total = total + self.rz[t]
+        return total
+
+
+def reduce_kernel(nt, cuts1, cuts, g1_ref, g2_ref, g3_ref, sm_ref, o1_ref, os_ref, o2_ref, o3_ref, om_ref, *rest):
+    here = place()
+    z, d, core, x, y = here
+    send, recv = rest[-2:]
+    sends = Sends(send, recv)
+    others = [{"tensor": lax.rem(z + dz, nt)} for dz in range(1, nt)]
+    others += [{"dp": xor_peer(core, x, y, k)} for k in (1, 2, 4)]
+    greet(others)
+    secs = [
+        Reduce(sends, nt, g, rest[10 * i : 10 * i + 10], c, here)
+        for i, (g, c) in enumerate(((g1_ref, cuts1), (g2_ref, cuts), (g3_ref, cuts)))
+    ]
+    small = SmallSum(sends, nt, sm_ref, rest[30:33], here)
+    for sec in secs:
+        sec.begin()
+    small.begin()
+    for sec in secs:
+        sec.first()
+    small.step(1)
+    for sec in secs:
+        sec.second()
+    small.step(2)
+    for sec in secs:
+        sec.third()
+    small.step(3)
+    total = secs[0].last()
+    width = o1_ref.shape[1]
+    o1_ref[...] = total[:, :width]
+    os_ref[...] = total[:, width:]
+    o2_ref[...] = secs[1].last()
+    o3_ref[...] = secs[2].last()
+    om_ref[...] = small.last()
+    sends.finish()
+
+
+def call(kernel, outs, scratch, *args, name, collective_id=None):
+    params = dict(vmem_limit_bytes=VMEM_LIMIT)
+    if collective_id is not None:
+        params.update(collective_id=collective_id, has_side_effects=True)
     return pl.pallas_call(
         kernel,
         out_shape=[jax.ShapeDtypeStruct(s, d) for s, d in outs],
         in_specs=[pl.BlockSpec(memory_space=pltpu.VMEM)] * len(args),
         out_specs=[pl.BlockSpec(memory_space=pltpu.VMEM)] * len(outs),
-        scratch_shapes=[pltpu.VMEM(s, d) for s, d in scratch],
-        compiler_params=pltpu.CompilerParams(vmem_limit_bytes=VMEM_LIMIT),
+        scratch_shapes=[s if not isinstance(s, tuple) else pltpu.VMEM(*s) for s in scratch],
+        compiler_params=pltpu.CompilerParams(**params),
         name=name,
     )(*args)
+
+
+def semaphores(n):
+    return [pltpu.SemaphoreType.DMA((n,)), pltpu.SemaphoreType.DMA((n,))]
 
 
 def shifted(v, axis, by):
     n = lax.axis_size(axis)
     return lax.ppermute(v, axis, [(i, i + by) for i in range(n) if 0 <= i + by < n])
+
+
+def gather_all(nt, nd, w1, w2, w3, ws, par, edge):
+    rows = ws.shape[0]
+    if nd == 8:
+        full = lambda w: ((rows * nd, w.shape[1] * nt), BF16)
+        return call(
+            functools.partial(gather_kernel, nt),
+            [full(w1), full(w2), full(w3), ((rows * nd, ws.shape[1]), BF16), ((nt, *par.shape), F32), (edge.shape, BF16)],
+            semaphores(3 * Gather.MESSAGES + 7 + nt) + [pltpu.SemaphoreType.DMA((5,))],
+            w1, w2, w3, ws, par, edge, name="gather", collective_id=0,
+        )
+    both = ("tensor", "dp")
+    pack = lax.all_gather(jnp.concatenate([w1, w2, w3], axis=1), both, axis=0).reshape(nt, nd * rows, -1)
+    out, at = [], 0
+    for w in (w1, w2, w3):
+        k = w.shape[1]
+        out.append(pack[:, :, at : at + k].transpose(1, 0, 2).reshape(nd * rows, nt * k))
+        at += k
+    out.append(lax.all_gather(ws, "dp", axis=0, tiled=True))
+    out.append(lax.all_gather(par, "tensor", axis=0))
+    return (*out, shifted(edge, "tensor", 1))
+
+
+def chain(nt, by, mine, whole):
+    seqs, state, di = mine.shape
+    return call(
+        functools.partial(chain_kernel, nt, by),
+        [(mine.shape, BF16)],
+        [(mine.shape, BF16)] + semaphores(seqs * di // WIDE),
+        mine, whole, name="states" if by > 0 else "states_back", collective_id=1 if by > 0 else 2,
+    )[0]
+
+
+def reduce_all(nt, nd, g1, g2, g3, sm, sh):
+    dim = g1.shape[0]
+    rows = dim // nd
+    part = (g1.shape[1] - sh) // nt
+    dcol = g2.shape[1] // nt
+    if nd == 8:
+        cuts1 = ((0, part, True), (part * nt, sh, False))
+        cuts = ((0, dcol, True),)
+        scratch = []
+        for g, w in ((g1, part + sh), (g2, dcol), (g3, dcol)):
+            scratch += Reduce.scratch(rows, g.shape[1], nt, w)
+        scratch += SmallSum.scratch(sm.shape, nt)
+        count = 3 * Reduce.MESSAGES + SmallSum.MESSAGES
+        return call(
+            functools.partial(reduce_kernel, nt, cuts1, cuts),
+            [((rows, part), F32), ((rows, sh), F32), ((rows, dcol), F32), ((rows, dcol), F32), (sm.shape, F32)],
+            scratch + semaphores(count),
+            g1, g2, g3, sm, name="reduce", collective_id=3,
+        )
+    both = ("tensor", "dp")
+    parts = [g[:, : nt * w].reshape(dim, nt, w).transpose(1, 0, 2) for g, w in ((g1, part), (g2, dcol), (g3, dcol))]
+    big = jnp.concatenate(parts, axis=2).reshape(nt * nd, rows, -1)
+    big = lax.psum_scatter(big, both, scatter_dimension=0).astype(F32)
+    shared = g1[:, nt * part :].reshape(nd, rows, sh).astype(F32)
+    shared = lax.psum(lax.psum_scatter(shared, "dp", scatter_dimension=0), "tensor")
+    return big[:, :part], shared, big[:, part : part + dcol], big[:, part + dcol :], lax.psum(sm, both)
 
 
 def local(
@@ -478,7 +917,6 @@
 ):
     nt = lax.axis_size("tensor")
     nd = lax.axis_size("dp")
-    both = ("tensor", "dp")
     me = lax.axis_index("tensor")
     seqs, span, dim = block_input.shape
     tokens = seqs * span
@@ -491,21 +929,19 @@
     heads = hloc * nt
 
     delta_w = lax.dynamic_update_slice(jnp.zeros((rows, 128), BF16), input_delta_weight, (0, me * hloc))
-    pack = jnp.concatenate(
-        [input_gate_inner_weight[:, 1], input_gate_inner_weight[:, 0], output_projection_weight.T, delta_w], axis=1
+    w1 = jnp.concatenate([input_gate_inner_weight[:, 1], delta_w], axis=1)
+    w2 = input_gate_inner_weight[:, 0]
+    w3 = output_projection_weight.T
+    head = jnp.stack([decay_log, delta_bias, skip_gain])
+    par = jnp.concatenate([
+        conv_inner.astype(F32), shift_inner.astype(F32)[None], gated_gain[None], jnp.zeros((2, dcol), F32),
+        jnp.pad(head, ((0, 5), (0, dcol - hloc)))], axis=0)
+    w1, w2, w3, ws, par, xh = gather_all(
+        nt, nd, w1, w2, w3, input_shared_weight, par, block_input[:, span - 16 :].reshape(seqs * 16, dim)
     )
-    full = lax.all_gather(pack, both, axis=0).reshape(nt, dim, 3 * dcol + 128)
-    wi, wg, wo = (full[:, :, dcol * k : dcol * (k + 1)].transpose(1, 0, 2).reshape(dim, di) for k in range(3))
-    wd = jnp.sum(full[:, :, 3 * dcol :].astype(F32), axis=0).astype(BF16)
-    ws = lax.all_gather(input_shared_weight, "dp", axis=0, tiled=True)
-    wsd = jnp.concatenate([ws, wd], axis=1)
-    chan = jnp.concatenate([conv_inner.astype(F32), shift_inner.astype(F32)[None], gated_gain[None]], axis=0)
-    head = jnp.stack([decay_log, delta_bias, skip_gain])
-    par = jnp.concatenate([chan, jnp.pad(head, ((0, 3), (0, dcol - hloc)))], axis=0)
-    par = lax.all_gather(par, "tensor", axis=0)
-    chan = par[:, :6].transpose(1, 0, 2).reshape(6, di)
-    head = par[:, 6:9, :hloc].transpose(1, 0, 2).reshape(3, heads)
-    ti = jnp.pad(chan[:5], ((0, 3), (0, 0)))
+    chan = par[:, :8].transpose(1, 0, 2).reshape(8, di)
+    head = par[:, 8:11, :hloc].transpose(1, 0, 2).reshape(3, heads)
+    ti = chan
     ts = jnp.pad(jnp.concatenate([conv_shared.astype(F32), shift_shared.astype(F32)[None]], axis=0), ((0, 3), (0, 0)))
     ak = -jnp.exp(head[0])
     dpar = jnp.pad(jnp.stack([head[1], ak * LOG2E, ak]), ((0, 5), (0, 128 - heads)))
@@ -523,42 +959,37 @@
 
     x = block_input.reshape(tokens, dim)
     c = cotangent.reshape(tokens, dim)
-    xh = shifted(block_input[:, span - 16 :], "tensor", 1).reshape(seqs * 16, dim)
 
     h, rawi, raws, xs, bc, draw, acs, bs, fresh, dec = call(
-        functools.partial(front_kernel, heads),
+        functools.partial(front_kernel, heads, nt),
         [((tokens, dim), BF16), ((seqs, span + 16, di), F32), ((seqs, span + 16, sh), F32), ((tokens, di), BF16),
          ((tokens, sh), BF16), ((tokens, 128), F32), ((tokens, 128), F32), ((tokens, 128), F32),
          ((blocks, state, di), F32), ((blocks, 8, di), F32)],
         [((seqs * 16, dim), BF16), ((SPAN, 128), BF16)],
-        x, xh, gain, wi, wsd, ti, ts, dpar, sel, tri, name="front",
+        x, xh, gain, w1, ws, ti, ts, dpar, sel, tri, name="front",
     )
 
     fr = fresh.reshape(seqs, blocks // seqs, state, di)
-    de = dec.reshape(seqs, blocks // seqs, 8, di)[:, :, 0:1]
+    de = dec.reshape(seqs, blocks // seqs, 8, di)
     whole, mine = de[:, 0], fr[:, 0]
     for j in range(1, blocks // seqs):
-        mine = de[:, j] * mine + fr[:, j]
+        mine = de[:, j, 0:1] * mine + fr[:, j]
         whole = de[:, j] * whole
-    sin = jnp.zeros((seqs, state, di), BF16)
-    for _ in range(nt - 1):
-        sin = shifted((mine + whole * sin.astype(F32)).astype(BF16), "tensor", 1)
-
-    out, yn, dgate, dy, rr, vv, ggg, skg, go = call(
+    sin = chain(nt, 1, mine, whole)
+
+    out, yn, dgate, dy, rr, vv, ggg, skg, g3 = call(
         functools.partial(mid_kernel, heads),
         [((tokens, dim), BF16), ((tokens, di), BF16), ((tokens, di), BF16), ((tokens, di), BF16), ((tokens, 128), F32),
          ((blocks, state, di), F32), ((8, di), F32), ((8, 128), F32), ((dim, di), BF16)],
         [((SPAN, di), F32)] * 4 + [((128, SPAN), F32)] * 2 + [((SPAN, 128), BF16)],
-        x, c, h, wg, wo, ggain, skip, xs, bc, acs, bs, sin, fresh, dec, sel, selt, name="mid",
+        x, c, h, w2, w3, ggain, skip, xs, bc, acs, bs, sin, fresh, dec, sel, selt, name="mid",
     )
 
     vr = vv.reshape(seqs, blocks // seqs, state, di)
     mine = vr[:, blocks // seqs - 1]
     for j in range(blocks // seqs - 2, -1, -1):
-        mine = de[:, j] * mine + vr[:, j]
-    ds = jnp.zeros((seqs, state, di), BF16)
-    for _ in range(nt - 1):
-        ds = shifted((mine + whole * ds.astype(F32)).astype(BF16), "tensor", -1)
+        mine = de[:, j, 0:1] * mine + vr[:, j]
+    ds = chain(nt, -1, mine, whole)
 
     dpi, dps, dd, small, tgi, tgs = call(
         functools.partial(back_kernel, heads),
@@ -571,39 +1002,40 @@
 
     hi = shifted(dpi.reshape(seqs, span, di)[:, :8], "tensor", -1)
     hs = shifted(dps.reshape(seqs, span, sh)[:, :8], "tensor", -1)
-    ig, gi, gg, gsd, ng = call(
-        last_kernel,
-        [((tokens, dim), BF16), ((dim, di), BF16), ((dim, di), BF16), ((dim, sh + 128), BF16), ((8, dim), F32)],
-        [((tokens, di), BF16), ((tokens, sh + 128), BF16)],
-        x, c, gain, h, dpi, dps, hi, hs, dd, dgate, ti, ts, wi, wg, wsd, name="last",
+    ig, g1, g2, ng = call(
+        functools.partial(last_kernel, nt),
+        [((tokens, dim), BF16), ((dim, w1.shape[1] + sh), BF16), ((dim, di), BF16), ((8, dim), F32)],
+        [((tokens, w1.shape[1] + sh), BF16)],
+        x, c, gain, h, dpi, dps, hi, hs, dd, dgate, ti, ts, w1, w2, ws, name="last",
     )
 
-    parts = [g.reshape(dim, nt, dcol).transpose(1, 0, 2) for g in (gg, gi, go)]
-    big = jnp.concatenate(parts, axis=2).reshape(nt * nd, rows, 3 * dcol)
-    mine = lax.psum_scatter(big, both, scatter_dimension=0).astype(F32)
-    gate_inner_grad = mine[:, : 2 * dcol].reshape(rows, 2, dcol)
-    out_weight_grad = mine[:, 2 * dcol :].T
-    gsd = lax.psum_scatter(gsd.reshape(nd, rows, sh + 128).astype(F32), "dp", scatter_dimension=0)
-    gsd = lax.psum(gsd, "tensor")
-    tgi, ggg, tgs, ng, small, skg = lax.psum((tgi, ggg, tgs, ng, small, skg), both)
-    cut = lambda v: lax.dynamic_slice_in_dim(v, me * dcol, dcol, axis=-1)
-    hcut = lambda v: lax.dynamic_slice_in_dim(v, me * hloc, hloc, axis=-1)
+    sm = jnp.concatenate([
+        tgi[:5].reshape(-1), ggg[0], ng[0], tgs[:5].reshape(-1), small[0], small[1], skg[0],
+        jnp.zeros(8 * di - 6 * di - dim - 5 * sh - 3 * 128, F32)]).reshape(8, di)
+    g1, gs, g2, g3, sm = reduce_all(nt, nd, g1, g2, g3, sm, sh)
+    sm = sm.reshape(-1)
+    cut = lambda k: lax.dynamic_slice_in_dim(sm, k * di + me * dcol, dcol)
+    at = 6 * di
+    ng = sm[at : at + dim]
+    tgs = sm[at + dim : at + dim + 5 * sh].reshape(5, sh)
+    at = at + dim + 5 * sh
+    hcut = lambda k: lax.dynamic_slice_in_dim(sm, at + 128 * k + me * hloc, hloc)
     return (
         out.reshape(block_input.shape),
         ig.reshape(block_input.shape),
-        ng[0],
-        gate_inner_grad,
-        gsd[:, :sh],
-        hcut(gsd[:, sh:]),
-        cut(tgi[:4]),
-        cut(tgi[4]),
+        ng,
+        jnp.stack([g2, g1[:, :dcol]], axis=1),
+        gs,
+        lax.dynamic_slice_in_dim(g1[:, dcol:], me * hloc, hloc, axis=1),
+        jnp.stack([cut(k) for k in range(4)]),
+        cut(4),
         tgs[:4],
         tgs[4],
-        hcut(small[0]),
-        hcut(small[1]),
-        hcut(skg[0]),
-        cut(ggg[0]),
-        out_weight_grad,
+        hcut(0),
+        hcut(1),
+        hcut(2),
+        cut(5),
+        g3.T,
     )
 
 

time: 725 us -> 373 us (0.51); the launches traced: 713 us -> 372 us
  waiting for transfers between devices: 436 us -> 2.34 us
  Pallas kernels: 129 us -> 320 us
  local copies, waits for them, and re-layouts: 65.1 us -> 30.4 us
  blocking collectives: 23.5 us -> 0 us
  starting transfers between devices: 24.4 us -> 2.82 us
  between operations: 14.4 us -> 0.87 us
    pallas_call x4 -> x8, Pallas kernels: 129 us -> 320 us  [call(): pl.pallas_call(kernel, out_shape=[jax.ShapeDtypeStruct(s, d) for s, d in...]
    psum x2 -> x0, waiting for transfers between devices: 152 us -> none  [the longest x1 122 us: local(): lax.psum((tgi, ggg, tgs, ng, small, skg), both)]
    reduce_scatter x2 -> x0, waiting for transfers between devices: 145 us -> none  [the longest x1 122 us: local(): mine = lax.psum_scatter(big, both, scatter_dimension=0).astype(F32)]
    ppermute x9 -> x2, waiting for transfers between devices: 93.2 us -> 2.34 us  [shifted(): lax.ppermute(v, axis, [(i, i + by) for i in range(n) if 0 <= i + by < n])]
    all_gather x1 -> x0, waiting for transfers between devices: 44.9 us -> none  [local(): full = lax.all_gather(pack, both, axis=0).reshape(nt, dim, 3 * dcol + 128)]
    all_gather x2 -> x0, blocking collectives: 23.5 us -> none  [the longest x1 13.9 us: local(): par = lax.all_gather(par, 'tensor', axis=0)]
    ppermute x9 -> x2, starting transfers between devices: 24.2 us -> 2.82 us  [shifted(): lax.ppermute(v, axis, [(i, i + by) for i in range(n) if 0 <= i + by < n])]
    reshape x4, local copies, waits for them, and re-layouts: 15.5 us -> 2.94 us  [the longest x1 0.81 us: local(): tgi[:5].reshape(-1)]
  transfers between devices with their start and end apart: 14 -> 2, of which waited for: 12 -> 1; matrix products, arithmetic and copies ran while one was open for 9% -> 1% of each run, Pallas kernels for 0% -> 0%
where the time goes in v2:
time: 373 us; the launch traced here: 372 us
  Pallas kernels  320 us (86%)
  local copies, waits for them, and re-layouts  30.4 us (8%)
  other arithmetic  15 us (4%)
    pallas_call x8, Pallas kernels, call(): pl.pallas_call(kernel, out_shape=[jax.ShapeDtypeStruct(s, d) for s, d in...  320 us
  transfers between devices with their start and end apart: 2, of which 1 were waited for; matrix products, arithmetic and copies ran while one was open for 1% of the time, Pallas kernels for 0%

profile of v2, /device:TPU:0, one launch (start us, length us, event | category | flops | bytes accessed | tf_op | source)
XLA Modules:
  0.0 371.9 jit_solution(9683185804050224560)
XLA Ops:
  0.7 0.8 copy.36
  1.5 1.2 fusion.19
  2.7 1.4 slice.112
  7.7 1.9 concatenate.14.par_ref
  9.6 53.0 %gather.1 = (bf16[768,2048]{1,0:T(8,128)(2,1)}, bf16[768,1536]{1,0:T(8,128)(2,1)}, bf16[768,1536]{1,0:T(8,128)(2,1)}, bf16[768,256]{1,0:T(8,128)(2,1)}, f32[4,16,384]{2,1,0:T(8,128)}, /*index=5*/bf16[32,768]{1,0:T(8,128)(2,1)}) custom-call(bf16[96,512]{1,0:T(8,128)(2,1)} %pad_maximum_fusion.1.w1_ref, bf16[96,384]{1,0:T(8,128)(2,1)} %get-tuple-element.141.w2_ref, ...), custom_call_target="tpu_custom_call" | custom-call | tf_op jit(solution)/shard_map/gather/pallas_call | solution.py:834
  63.4 1.4 slice_bitcast_fusion.8
  67.6 1.0 and_convert_fusion.sel_ref
  68.5 27.0 %front.1 = (bf16[1024,768]{1,0:T(8,128)(2,1)}, f32[2,528,1536]{2,1,0:T(8,128)}, f32[2,528,256]{2,1,0:T(8,128)}, bf16[1024,1536]{1,0:T(8,128)(2,1)}, bf16[1024,25...) custom-call(bf16[1024,768]{1,0:T(8,128)(2,1)} %bitcast.84, ...), custom_call_target="tpu_custom_call" | custom-call | tf_op jit(solution)/shard_map/front/pallas_call | solution.py:834
  95.5 1.0 fusion.18
  96.5 1.6 fusion.8.whole_ref
  98.1 1.0 fusion.4.selt_ref
  100.6 3.3 fusion.2.mine_ref
  103.8 26.9 %states.1.sin_ref = bf16[2,128,1536]{2,1,0:T(8,128)(2,1)} custom-call(f32[2,128,1536]{2,1,0:T(8,128)} %fusion.2.mine_ref, f32[2,8,1536]{2,1,0:T(8,128)} %fusion.8.whole_ref), custom_call_target="tpu_custom_call" | custom-call | tf_op jit(solution)/shard_map/states/pallas_call | solution.py:834
  130.8 36.2 %mid.1 = (bf16[1024,768]{1,0:T(8,128)(2,1)}, bf16[1024,1536]{1,0:T(8,128)(2,1)}, bf16[1024,1536]{1,0:T(8,128)(2,1)}, bf16[1024,1536]{1,0:T(8,128)(2,1)}, f32[102...) custom-call(bf16[1024,768]{1,0:T(8,128)(2,1)} %bitcast.85, ...), custom_call_target="tpu_custom_call" | custom-call | tf_op jit(solution)/shard_map/mid/pallas_call | solution.py:834
  167.0 3.3 fusion.mine_ref
  170.2 39.6 %states_back.1.ds_ref = bf16[2,128,1536]{2,1,0:T(8,128)(2,1)} custom-call(f32[2,128,1536]{2,1,0:T(8,128)} %fusion.mine_ref, f32[2,8,1536]{2,1,0:T(8,128)} %fusion.8.whole_ref), custom_call_target="tpu_custom_call" | custom-call | tf_op jit(solution)/shard_map/states_back/pallas_call | solution.py:834
  209.8 43.8 %back.1 = (f32[1024,1536]{1,0:T(8,128)}, f32[1024,256]{1,0:T(8,128)}, bf16[1024,128]{1,0:T(8,128)(2,1)}, f32[8,128]{1,0:T(8,128)}, f32[8,1536]{1,0:T(8,128)}, /*index=5*/f32[8,256]{1,0:T(8,128)}) custom-call(bf16[1024,1536]{1,0:T(8,128)(2,1)} %get-tuple-element.61.xs_ref, bf16[1024,256]{1,0:T(8,128)(2,1)} %get-tuple-element.62.bc_ref, ...), custom_call_target="tpu_custom_call" | custom-call | tf_op jit(solution)/shard_map/back/pallas_call | solution.py:834
  253.7 0.9 slice.156
  254.6 1.3 collective-permute-start
  256.6 1.5 collective-permute-start.1
  258.1 0.8 reshape.171
  258.9 0.8 slice_reduce_fusion
  260.5 2.3 collective-permute-done.1.hs_ref
  263.5 23.7 %last.1 = (bf16[1024,768]{1,0:T(8,128)(2,1)}, bf16[768,2304]{1,0:T(8,128)(2,1)}, bf16[768,1536]{1,0:T(8,128)(2,1)}, f32[8,768]{1,0:T(8,128)}) custom-call(bf16[1024,768]{1,0:T(8,128)(2,1)} %bitcast.86, bf16[1024,768]{1,0:T(8,128)(2,1)} %bitcast.90, f32[1,768]{1,0:T(1,128)} %broadcast_in_dim.40.gain_ref, bf16[1024,768]{1,0:T(8,128)(2,1)} %get-tuple-element.58.h_ref, ...), custom_call_target="tpu_custom_call" | custom-call | tf_op jit(solution)/shard_map/last/pallas_call | solution.py:834
  287.1 0.8 slice_reduce_fusion.1
  290.6 70.3 %reduce.17 = (f32[96,512]{1,0:T(8,128)}, f32[96,256]{1,0:T(8,128)}, f32[96,384]{1,0:T(8,128)}, f32[96,384]{1,0:T(8,128)}, f32[8,1536]{1,0:T(8,128)}) custom-call(bf16[768,2304]{1,0:T(8,128)(2,1)} %get-tuple-element.79.g1_ref, bf16[768,1536]{1,0:T(8,128)(2,1)} %get-tuple-element.80.g2_ref, bf16[768,1536]{1,0:T(8,128)(2,1)} %get-tuple-element.81.g3_ref, ...), custom_call_target="tpu_custom_call" | custom-call | tf_op jit(solution)/shard_map/reduce/pallas_call | solution.py:834
  360.9 1.0 slice_bitcast_fusion.4
  361.9 0.8 slice.140
  362.7 0.8 reshape.174
  363.5 0.8 slice.141
  366.1 0.9 pad_maximum_fusion
  367.1 0.9 copy.44
  (68 shorter events, 18.9 us)
Async XLA Ops:
  0.6 65.1 %copy-start.6 = (bf16[256]{0:T(256)(128)(2,1)S(1)}, bf16[256]{0:T(256)(128)(2,1)}, u32[]{:S(2)}) copy-start(bf16[256]{0:T(256)(128)(2,1)} %param.23) | copy-start | bytes 1540
  0.7 65.1 %copy-start.4 = (f32[768]{0:T(1024)S(1)}, f32[768]{0:T(1024)}, u32[]{:S(2)}) copy-start(f32[768]{0:T(1024)} %param.16) | copy-start | bytes 9220
  0.7 66.3 %copy-start.5 = (bf16[4,256]{1,0:T(4,128)(2,1)S(1)}, bf16[4,256]{1,0:T(4,128)(2,1)}, u32[]{:S(2)}) copy-start(bf16[4,256]{1,0:T(4,128)(2,1)} %param.22) | copy-start | bytes 6148
  254.6 8.3 %collective-permute-start = (f32[2,8,1536]{2,1,0:T(8,128)S(1)}, f32[2,8,1536]{2,1,0:T(8,128)S(1)}, u32[]{:S(2)}, u32[]{:S(2)}) collective-permute-start(f32[2,8,1536]{2,1,0:T(8,128)S(1)} %slice.156), channel_id=1, source_target_pairs={{1,0},{2,1},{3,2},{5,4},{6,5},{7,6},{9,8},{10,9},{11,10},{13,12},{... | collective-permute-start | bytes 294920 | tf_op jit(solution)/shard_map/ppermute | solution.py:851
  256.6 6.2 %collective-permute-start.1 = (f32[2,8,256]{2,1,0:T(8,128)S(1)}, f32[2,8,256]{2,1,0:T(8,128)S(1)}, u32[]{:S(2)}, u32[]{:S(2)}) collective-permute-start(f32[2,8,256]{2,1,0:T(8,128)S(1)} %slice.157), channel_id=1, source_target_pairs={{1,0},{2,1},{3,2},{5,4},{6,5},{7,6},{9,8},{10,9},{11,10},{13,12},{... | collective-permute-start | bytes 49160 | tf_op jit(solution)/shard_map/ppermute | solution.py:851
  262.8 0.6 copy-start.3
  262.8 0.6 copy-start.1
  360.9 9.7 %copy-start.2 = (f32[96,256]{1,0:T(8,128)S(1)}, f32[96,256]{1,0:T(8,128)}, u32[]{:S(2)}) copy-start(f32[96,256]{1,0:T(8,128)} %get-tuple-element.164) | copy-start | bytes 294916
  360.9 10.3 %copy-start = (f32[96,384]{1,0:T(8,128)S(1)}, f32[96,384]{1,0:T(8,128)}, u32[]{:S(2)}) copy-start(f32[96,384]{1,0:T(8,128)} %get-tuple-element.92) | copy-start | bytes 442372
